TPU v7x, 1024 devices: a whole 4x4x32 slice. The times are simulated.
1024 devices in a mesh: row: 64 (over y, z_hi, x), col: 16 (over z_lo, core).
Axes of the slice: x: 4, y: 4, z: 32 (z_hi: 4, z_lo: 8; z = z_hi * 8 + z_lo), core: 2. Of those that a mesh axis runs over, the one named last changes fastest.
Arguments:
- vectors: bfloat16 [8, 1048576], P(None, ('row', 'col')), may hold values from -6 to 6
- tile_blocks: bfloat16 [64, 16, 16, 256, 256], P('row', 'col'), may hold values from -0.375 to 0.375
- block_pairs: int32 [64, 16, 16, 2], P('row', 'col'), may hold values from 0 to 63
- tile_counts: int32 [64, 16], P('row', 'col'), may hold values from 2 to 16, as said below
Outputs:
- product: float32 [8, 1048576], P(None, ('row', 'col'))
Inputs may be any that keep to these rules, and one draw needn't show every extreme that they name: `tile_counts`: some tile (r, c) with r + c < 64 has exactly 16 live slots.
All inputs are finite; a program needn't handle non-finite values.
Results may differ from a plain program's by a relative error of at most 0.0003.
Values may be sent and summed in bfloat16 or wider, within the bound.
No kernel may reach another device: no remote copies, remote signals or barrier semaphores. Data moves between devices by JAX's collectives and lax.ppermute only.
A program may use at most 64 MiB of HBM per device.

v0:
```python
import jax
import jax.numpy as jnp
from jax import lax
from jax.sharding import PartitionSpec as P


def shifted_2(array, axis, by):
    devices = lax.axis_size(axis)
    pairs = [(i, i + by) for i in range(devices) if 0 <= i + by < devices]
    return lax.ppermute(array, axis, pairs)


def tile_terms(blocks, block_pairs, live_slots, near_blocks, far_blocks, block_count):
    near_rows = near_blocks[:, block_pairs[:, 1]]
    far_rows = far_blocks[:, block_pairs[:, 0]]
    normal = jnp.einsum("vka,kba->vkb", near_rows, blocks, preferred_element_type=jnp.float32)
    transposed = jnp.einsum("vkb,kba->vka", far_rows, blocks, preferred_element_type=jnp.float32)
    block_range = jnp.arange(block_count, dtype=jnp.int32)[None, :]
    place_row = jnp.where(
        (block_pairs[:, 0:1] == block_range) & live_slots[:, None], 1.0, 0.0
    ).astype(jnp.float32)
    place_col = jnp.where(
        (block_pairs[:, 1:2] == block_range) & live_slots[:, None], 1.0, 0.0
    ).astype(jnp.float32)
    normal_part = jnp.einsum("kn,vkb->vnb", place_row, normal, precision=lax.Precision.HIGHEST)
    trans_part = jnp.einsum("kn,vka->vna", place_col, transposed, precision=lax.Precision.HIGHEST)
    return (normal_part, trans_part)


def body(vectors, tile_blocks, block_pairs, tile_counts):
    row_count = lax.axis_size("row")
    col_count = lax.axis_size("col")
    col_index = lax.axis_index("col")
    row_index = lax.axis_index("row")
    digit_count = col_count.bit_length() - 1
    segment = lax.all_gather(vectors, "col", axis=1, tiled=True)
    vec_count = segment.shape[0]
    length = segment.shape[1]
    tile_width = tile_blocks.shape[-1]
    block_count = length // tile_width
    near_blocks = segment.reshape(vec_count, block_count, tile_width)
    blocks = tile_blocks[0, 0]
    pair_table = block_pairs[0, 0]
    tile_count = tile_counts[0, 0]
    in_band = row_index + col_index < row_count
    slot_count = blocks.shape[0]
    far_segment = segment
    for bit_number in range(digit_count):
        shifted = shifted_2(far_segment, "row", -(1 << bit_number))
        far_segment = jnp.where(col_index >> bit_number & 1 == 1, shifted, far_segment)
    far_blocks = far_segment.reshape(vec_count, block_count, tile_width)
    live_slots = (jnp.arange(slot_count, dtype=jnp.int32) < tile_count) & in_band
    normal_part, trans_part = tile_terms(
        blocks, pair_table, live_slots, near_blocks, far_blocks, block_count
    )
    arriving = normal_part.reshape(vec_count, length)
    for bit_number in range(digit_count):
        shifted = shifted_2(arriving, "row", 1 << bit_number)
        arriving = jnp.where(col_index >> bit_number & 1 == 1, shifted, arriving)
    combined = arriving + trans_part.reshape(vec_count, length)
    return lax.psum_scatter(combined, "col", scatter_dimension=1, tiled=True)


def solution(mesh):
    in_specs = (
        P(None, ("row", "col")),
        P("row", "col", None, None, None),
        P("row", "col", None, None),
        P("row", "col"),
    )
    out_specs = P(None, ("row", "col"))
    return jax.shard_map(body, mesh=mesh, in_specs=in_specs, out_specs=out_specs, check_vma=False)
```

profile of v0, /device:TPU:4, one launch (start us, length us, event | category | flops | bytes accessed | tf_op | source)
XLA Modules:
  0.0 651.7 jit_solution(6184708755151696940)
XLA Ops:
  6.5 0.0 copy-start
  6.5 0.0 reduce-scatter.2.cloned.1.call-start
  6.5 37.5 %all_gather.3 = bf16[8,16384]{1,0:T(8,128)(2,1)S(1)} all-gather(bf16[8,1024]{1,0:T(8,128)(2,1)} %param.4), channel_id=1, replica_groups=mesh['row'=64,'col'=16] {'col'}, dimensions={1}, use_global_device_ids=true | all-gather | bytes 278528 | tf_op jit(solution)/shard_map/all_gather | solution.py:36
  44.1 2.4 collective-permute-start.4
  47.2 0.8 slice_bitcast_fusion
  48.0 0.6 gather_fusion
  48.5 0.0 copy-done
  48.5 0.6 fusion.2
  49.2 0.7 convolution_bitcast_fusion.1
  49.9 0.3 copy.7
  50.2 3.4 collective-permute-start
  53.6 1.0 collective-permute-done.4
  54.7 4.0 collective-permute-start.5
  58.7 7.7 %collective-permute-done = f32[8,16384]{1,0:T(8,128)S(1)} collective-permute-done((f32[8,16384]{1,0:T(8,128)S(1)}, f32[8,16384]{1,0:T(8,128)S(1)}, u32[]{:S(2)}, u32[]{:S(2)}) %collective-permute-start) | collective-permute-done | bytes 524320 | tf_op jit(solution)/shard_map/ppermute | solution.py:10
  66.4 0.1 broadcast_select_fusion.1
  66.4 134.0 %collective-permute-start.1 = (f32[8,16384]{1,0:T(8,128)S(1)}, f32[8,16384]{1,0:T(8,128)S(1)}, u32[]{:S(2)}, u32[]{:S(2)}) collective-permute-start(f32[8,16384]{1,0:T(8,128)S(1)} %broadcast_select_fusion.1), channel_id=1, source_target_pairs={{0,32},{16,48},{32,64},{48,80},{64,96},{80,112},{96,128},{112,144}... | collective-permute-start | bytes 1572872 | tf_op jit(solution)/shard_map/ppermute | solution.py:10
  200.4 0.0 collective-permute-done.5
  200.5 1.3 collective-permute-start.6
  201.8 11.8 %collective-permute-done.1 = f32[8,16384]{1,0:T(8,128)S(1)} collective-permute-done((f32[8,16384]{1,0:T(8,128)S(1)}, f32[8,16384]{1,0:T(8,128)S(1)}, u32[]{:S(2)}, u32[]{:S(2)}) %collective-permute-start.1) | collective-permute-done | bytes 524320 | tf_op jit(solution)/shard_map/ppermute | solution.py:10
  213.6 0.1 broadcast_select_fusion.3
  213.6 12.4 %collective-permute-start.2 = (f32[8,16384]{1,0:T(8,128)S(1)}, f32[8,16384]{1,0:T(8,128)S(1)}, u32[]{:S(2)}, u32[]{:S(2)}) collective-permute-start(f32[8,16384]{1,0:T(8,128)S(1)} %broadcast_select_fusion.3), channel_id=1, source_target_pairs={{0,64},{16,80},{32,96},{48,112},{64,128},{80,144},{96,160},{112,17... | collective-permute-start | bytes 1572872 | tf_op jit(solution)/shard_map/ppermute | solution.py:10
  226.0 0.0 collective-permute-done.6
  226.1 1.3 collective-permute-start.7
  227.4 78.4 %collective-permute-done.2 = f32[8,16384]{1,0:T(8,128)S(1)} collective-permute-done((f32[8,16384]{1,0:T(8,128)S(1)}, f32[8,16384]{1,0:T(8,128)S(1)}, u32[]{:S(2)}, u32[]{:S(2)}) %collective-permute-start.2) | collective-permute-done | bytes 524320 | tf_op jit(solution)/shard_map/ppermute | solution.py:10
  305.7 0.1 broadcast_select_fusion.5
  305.8 12.3 %collective-permute-start.3 = (f32[8,16384]{1,0:T(8,128)S(1)}, f32[8,16384]{1,0:T(8,128)S(1)}, u32[]{:S(2)}, u32[]{:S(2)}) collective-permute-start(f32[8,16384]{1,0:T(8,128)S(1)} %broadcast_select_fusion.5), channel_id=1, source_target_pairs={{0,128},{16,144},{32,160},{48,176},{64,192},{80,208},{96,224},{112... | collective-permute-start | bytes 1572872 | tf_op jit(solution)/shard_map/ppermute | solution.py:10
  318.1 5.3 collective-permute-done.7
  323.5 0.6 gather_fusion.1
  324.0 0.4 fusion
  324.4 0.7 convolution_bitcast_fusion
  325.1 0.3 copy.8
  325.4 59.0 %collective-permute-done.3 = f32[8,16384]{1,0:T(8,128)S(1)} collective-permute-done((f32[8,16384]{1,0:T(8,128)S(1)}, f32[8,16384]{1,0:T(8,128)S(1)}, u32[]{:S(2)}, u32[]{:S(2)}) %collective-permute-start.3) | collective-permute-done | bytes 524320 | tf_op jit(solution)/shard_map/ppermute | solution.py:10
  384.4 0.9 select_add_fusion
  385.3 0.0 reduce-scatter.2.cloned.1.call-update
  385.3 259.5 %reduce-scatter.2.cloned.1.call-done = f32[8,1024]{1,0:T(8,128)} async-done(((f32[8,16384]{1,0:T(8,128)}), f32[8,1024]{1,0:T(8,128)}) %reduce-scatter.2.cloned.1.call-update) | async-done | bytes 32784 | tf_op jit(solution)/shard_map/reduce_scatter | solution.py:61
  (7 shorter events, 0.1 us)
Async XLA Ops:
  6.5 42.0 %copy-start = (bf16[1,1,16,256,256]{4,3,2,1,0:T(8,128)(2,1)S(1)}, bf16[1,1,16,256,256]{4,3,2,1,0:T(8,128)(2,1)}, u32[]{:S(2)}) copy-start(bf16[1,1,16,256,256]{4,3,2,1,0:T(8,128)(2,1)} %param.5) | copy-start | bytes 6291460
  6.5 638.3 %reduce-scatter.2.cloned.1.call-start = ((), (), s32[]{:S(2)}) async-start(), calls=%async_computation.1 | async-start | bytes 557056 | tf_op jit(solution)/shard_map/reduce_scatter | solution.py:61
  44.1 10.5 %collective-permute-start.4 = (bf16[8,16384]{1,0:T(8,128)(2,1)S(1)}, bf16[8,16384]{1,0:T(8,128)(2,1)}, u32[]{:S(2)}, u32[]{:S(2)}) collective-permute-start(bf16[8,16384]{1,0:T(8,128)(2,1)S(1)} %all_gather.3), channel_id=1, source_target_pairs={{16,0},{32,16},{48,32},{64,48},{80,64},{96,80},{112,96},{128,112},... | collective-permute-start | bytes 786440 | tf_op jit(solution)/shard_map/ppermute | solution.py:10
  50.2 16.2 %collective-permute-start = (f32[8,16384]{1,0:T(8,128)S(1)}, f32[8,16384]{1,0:T(8,128)S(1)}, u32[]{:S(2)}, u32[]{:S(2)}) collective-permute-start(f32[8,16384]{1,0:T(8,128)S(1)} %bitcast.45), channel_id=1, source_target_pairs={{0,16},{16,32},{32,48},{48,64},{64,80},{80,96},{96,112},{112,128},... | collective-permute-start | bytes 1572872 | tf_op jit(solution)/shard_map/ppermute | solution.py:10
  54.7 145.8 %collective-permute-start.5 = (bf16[8,16384]{1,0:T(8,128)(2,1)S(1)}, bf16[8,16384]{1,0:T(8,128)(2,1)S(1)}, u32[]{:S(2)}, u32[]{:S(2)}) collective-permute-start(bf16[8,16384]{1,0:T(8,128)(2,1)S(1)} %broadcast_select_fusion), channel_id=1, source_target_pairs={{32,0},{48,16},{64,32},{80,48},{96,64},{112,80},{128,96},{144,112}... | collective-permute-start | bytes 786440 | tf_op jit(solution)/shard_map/ppermute | solution.py:10
  66.4 147.1 %collective-permute-start.1 = (f32[8,16384]{1,0:T(8,128)S(1)}, f32[8,16384]{1,0:T(8,128)S(1)}, u32[]{:S(2)}, u32[]{:S(2)}) collective-permute-start(f32[8,16384]{1,0:T(8,128)S(1)} %broadcast_select_fusion.1), channel_id=1, source_target_pairs={{0,32},{16,48},{32,64},{48,80},{64,96},{80,112},{96,128},{112,144}... | collective-permute-start | bytes 1572872 | tf_op jit(solution)/shard_map/ppermute | solution.py:10
  200.5 25.5 %collective-permute-start.6 = (bf16[8,16384]{1,0:T(8,128)(2,1)S(1)}, bf16[8,16384]{1,0:T(8,128)(2,1)S(1)}, u32[]{:S(2)}, u32[]{:S(2)}) collective-permute-start(bf16[8,16384]{1,0:T(8,128)(2,1)S(1)} %broadcast_select_fusion.2), channel_id=1, source_target_pairs={{64,0},{80,16},{96,32},{112,48},{128,64},{144,80},{160,96},{176,11... | collective-permute-start | bytes 786440 | tf_op jit(solution)/shard_map/ppermute | solution.py:10
  213.6 92.1 %collective-permute-start.2 = (f32[8,16384]{1,0:T(8,128)S(1)}, f32[8,16384]{1,0:T(8,128)S(1)}, u32[]{:S(2)}, u32[]{:S(2)}) collective-permute-start(f32[8,16384]{1,0:T(8,128)S(1)} %broadcast_select_fusion.3), channel_id=1, source_target_pairs={{0,64},{16,80},{32,96},{48,112},{64,128},{80,144},{96,160},{112,17... | collective-permute-start | bytes 1572872 | tf_op jit(solution)/shard_map/ppermute | solution.py:10
  226.1 97.3 %collective-permute-start.7 = (bf16[8,16384]{1,0:T(8,128)(2,1)S(1)}, bf16[8,16384]{1,0:T(8,128)(2,1)S(1)}, u32[]{:S(2)}, u32[]{:S(2)}) collective-permute-start(bf16[8,16384]{1,0:T(8,128)(2,1)S(1)} %broadcast_select_fusion.4), channel_id=1, source_target_pairs={{128,0},{144,16},{160,32},{176,48},{192,64},{208,80},{224,96},{240... | collective-permute-start | bytes 786440 | tf_op jit(solution)/shard_map/ppermute | solution.py:10
  305.8 78.6 %collective-permute-start.3 = (f32[8,16384]{1,0:T(8,128)S(1)}, f32[8,16384]{1,0:T(8,128)S(1)}, u32[]{:S(2)}, u32[]{:S(2)}) collective-permute-start(f32[8,16384]{1,0:T(8,128)S(1)} %broadcast_select_fusion.5), channel_id=1, source_target_pairs={{0,128},{16,144},{32,160},{48,176},{64,192},{80,208},{96,224},{112... | collective-permute-start | bytes 1572872 | tf_op jit(solution)/shard_map/ppermute | solution.py:10
Sparse Core Ops, SparseCore 0:
  385.5 259.3 reduce-scatter.1
where the time goes:
time: 652 us
  waiting for transfers between devices  423 us (65%)
  starting transfers between devices  171 us (26%)
  blocking collectives  37.5 us (6%)
  between operations  14.2 us (2%)
    reduce_scatter x1, waiting for transfers between devices, body(): return lax.psum_scatter(combined, 'col', scatter_dimension=1, tiled=True)  260 us
    ppermute x8, starting transfers between devices, shifted_2(): return lax.ppermute(array, axis, pairs)  171 us
    ppermute x8, waiting for transfers between devices, shifted_2(): return lax.ppermute(array, axis, pairs)  163 us
    all_gather x1, blocking collectives, body(): segment = lax.all_gather(vectors, 'col', axis=1, tiled=True)  37.5 us
  transfers between devices with their start and end apart: 9, of which 7 were waited for; matrix products, arithmetic and copies ran while one was open for 1% of the time, Pallas kernels for 0%

commit v1 on v0

v1 whole, which is shorter than its diff:
```python
import functools

import jax
import jax.numpy as jnp
from jax import lax
from jax.experimental import pallas as pl
from jax.experimental.pallas import tpu as pltpu
from jax.sharding import PartitionSpec as P


def place_of(block, own, digits, per_piece):
    mixed = (block // per_piece) ^ own
    turned = jnp.int32(0)
    for bit in range(digits):
        turned = turned | (((mixed >> bit) & 1) << (digits - 1 - bit))
    return turned * per_piece + block % per_piece


def pick_kernel(near_index, far_index, own_ref, segment, near_rows, far_rows, *, digits, per_piece):
    slots, _, width = near_rows.shape
    own = own_ref[0]
    for index, rows in ((far_index, far_rows), (near_index, near_rows)):
        for slot in range(slots):
            place = place_of(index[slot], own, digits, per_piece)
            rows[slot] = segment[:, pl.ds(pl.multiple_of(place * width, width), width)]


def add_kernel(near_index, far_index, own_ref, count_ref, trans, arrived, total, *, digits, per_piece):
    slots, _, width = trans.shape
    own = own_ref[0]
    count = count_ref[0]
    total[...] = jnp.zeros_like(total)
    for slot in range(slots):
        place = place_of(near_index[slot], own, digits, per_piece)
        where = pl.ds(pl.multiple_of(place * width, width), width)
        total[:, where] += jnp.where(slot < count, trans[slot], 0.0)
        place = place_of(far_index[slot], own, digits, per_piece)
        where = pl.ds(pl.multiple_of(place * width, width), width)
        total[:, where] += arrived[slot]


def body(vectors, tile_blocks, block_pairs, tile_counts):
    row_count = lax.axis_size("row")
    col_count = lax.axis_size("col")
    col_index = lax.axis_index("col")
    row_index = lax.axis_index("row")
    digits = col_count.bit_length() - 1
    blocks = tile_blocks[0, 0]
    pair_rows = block_pairs[0, 0, :, 0]
    pair_cols = block_pairs[0, 0, :, 1]
    slots, width, _ = blocks.shape
    vec_count, piece = vectors.shape
    per_piece = piece // width
    own = col_index.astype(jnp.int32)[None]
    in_band = row_index + col_index < row_count
    count = jnp.where(in_band, tile_counts[0, 0], 0)
    up = [(r * col_count + c, (r + c) * col_count + c)
          for r in range(row_count) for c in range(col_count) if r + c < row_count]
    down = [(b, a) for a, b in up]
    both = ("row", "col")

    far_index = lax.ppermute(pair_rows, both, up)
    segment = vectors
    for bit in reversed(range(digits)):
        pairs = [(c, c ^ (1 << bit)) for c in range(col_count)]
        segment = jnp.concatenate([segment, lax.ppermute(segment, "col", pairs)], axis=1)

    smem = pl.BlockSpec(memory_space=pltpu.SMEM)
    vmem = pl.BlockSpec(memory_space=pltpu.VMEM)
    rows_type = jax.ShapeDtypeStruct((slots, vec_count, width), vectors.dtype)
    near_rows, far_picked = pl.pallas_call(
        functools.partial(pick_kernel, digits=digits, per_piece=per_piece),
        out_shape=(rows_type, rows_type),
        in_specs=[smem, smem, smem, vmem],
        out_specs=(vmem, vmem),
    )(pair_cols, far_index, own, segment)
    far_rows = lax.ppermute(far_picked, both, down)
    live = (jnp.arange(slots) < count)[:, None, None]
    normal = jnp.einsum("kva,kba->kvb", near_rows, blocks, preferred_element_type=jnp.float32)
    normal = jnp.where(live, normal, 0.0)
    arrived = lax.ppermute(normal, both, up)
    trans = jnp.einsum("kvb,kba->kva", far_rows, blocks, preferred_element_type=jnp.float32)

    total = pl.pallas_call(
        functools.partial(add_kernel, digits=digits, per_piece=per_piece),
        out_shape=jax.ShapeDtypeStruct((vec_count, piece * col_count), jnp.float32),
        in_specs=[smem, smem, smem, smem, vmem, vmem],
        out_specs=vmem,
    )(pair_cols, far_index, own, count[None], trans, arrived)
    for bit in range(digits):
        pairs = [(c, c ^ (1 << bit)) for c in range(col_count)]
        half = total.shape[1] // 2
        total = total[:, :half] + lax.ppermute(total[:, half:], "col", pairs)
    return total


def solution(mesh):
    in_specs = (
        P(None, ("row", "col")),
        P("row", "col", None, None, None),
        P("row", "col", None, None),
        P("row", "col"),
    )
    out_specs = P(None, ("row", "col"))
    return jax.shard_map(body, mesh=mesh, in_specs=in_specs, out_specs=out_specs, check_vma=False)
```

time: 652 us -> 132 us (0.20)
  the two profiles are of different devices: /device:TPU:4 before, /device:TPU:26 now
where the time goes in v1:
time: 132 us; the launch traced here: 131 us
  starting transfers between devices  93.3 us (71%)
  waiting for transfers between devices  22 us (17%)
  local copies, waits for them, and re-layouts  4.43 us (3%)
  Pallas kernels  4.08 us (3%)
  other arithmetic  3.81 us (3%)
  matrix products  2.53 us (2%)
    ppermute x4, starting transfers between devices, body(): total = total[:, :half] + lax.ppermute(total[:, half:], 'col', pairs)  49.9 us
    ppermute x4, starting transfers between devices, body(): lax.ppermute(segment, 'col', pairs)  40.6 us
    ppermute x4, waiting for transfers between devices, body(): total = total[:, :half] + lax.ppermute(total[:, half:], 'col', pairs)  12.9 us
    ppermute x4, waiting for transfers between devices, body(): lax.ppermute(segment, 'col', pairs)  9.15 us
  transfers between devices with their start and end apart: 11, of which 8 were waited for; matrix products, arithmetic and copies ran while one was open for 4% of the time, Pallas kernels for 0%

profile of v1, /device:TPU:26, one launch (start us, length us, event | category | flops | bytes accessed | tf_op | source)
XLA Modules:
  0.0 131.0 jit_solution(12479775027000848153)
XLA Ops:
  0.0 0.0 copy-start
  0.0 1.4 %slice_bitcast_fusion = (s32[16]{0:T(128)S(1)}, s32[16]{0:T(128)}) fusion(s32[1,1,16,2]{2,3,1,0:T(2,128)} %param.6), kind=kLoop, calls=%fused_computation.18 | loop fusion | bytes 256 | tf_op jit(solution)/shard_map/squeeze | solution.py:49
  1.4 0.6 collective-permute-start
  2.0 32.6 %collective-permute-start.1 = (bf16[8,1024]{1,0:T(8,128)(2,1)}, bf16[8,1024]{1,0:T(8,128)(2,1)S(1)}, u32[]{:S(2)}, u32[]{:S(2)}) collective-permute-start(bf16[8,1024]{1,0:T(8,128)(2,1)} %param.4), channel_id=1, source_target_pairs={{0,8},{1,9},{2,10},{3,11},{4,12},{5,13},{6,14},{7,15},{8,0},{9,1},... | collective-permute-start | bytes 49160 | tf_op jit(solution)/shard_map/ppermute | solution.py:66
  34.6 0.7 constant_dynamic-update-slice_fusion.4
  36.0 0.5 collective-permute-done.1
  36.5 0.7 pad_maximum_fusion.2
  37.3 1.9 %collective-permute-start.2 = (bf16[8,2048]{1,0:T(8,128)(2,1)S(1)}, bf16[8,2048]{1,0:T(8,128)(2,1)S(1)}, u32[]{:S(2)}, u32[]{:S(2)}) collective-permute-start(bf16[8,2048]{1,0:T(8,128)(2,1)S(1)} %pad_maximum_fusion.2), channel_id=1, source_target_pairs={{0,4},{1,5},{2,6},{3,7},{4,0},{5,1},{6,2},{7,3},{8,12},{9,13},{10,... | collective-permute-start | bytes 98312 | tf_op jit(solution)/shard_map/ppermute | solution.py:66
  39.2 5.1 %collective-permute-done.2 = bf16[8,2048]{1,0:T(8,128)(2,1)S(1)} collective-permute-done((bf16[8,2048]{1,0:T(8,128)(2,1)S(1)}, bf16[8,2048]{1,0:T(8,128)(2,1)S(1)}, u32[]{:S(2)}, u32[]{:S(2)}) %collective-permute-start.2) | collective-permute-done | bytes 32800 | tf_op jit(solution)/shard_map/ppermute | solution.py:66
  44.3 0.7 pad_maximum_fusion.1
  45.0 4.1 %collective-permute-start.3 = (bf16[8,4096]{1,0:T(8,128)(2,1)S(1)}, bf16[8,4096]{1,0:T(8,128)(2,1)S(1)}, u32[]{:S(2)}, u32[]{:S(2)}) collective-permute-start(bf16[8,4096]{1,0:T(8,128)(2,1)S(1)} %pad_maximum_fusion.1), channel_id=1, source_target_pairs={{0,2},{1,3},{2,0},{3,1},{4,6},{5,7},{6,4},{7,5},{8,10},{9,11},{10,... | collective-permute-start | bytes 196616 | tf_op jit(solution)/shard_map/ppermute | solution.py:66
  49.2 2.2 %collective-permute-done.3 = bf16[8,4096]{1,0:T(8,128)(2,1)S(1)} collective-permute-done((bf16[8,4096]{1,0:T(8,128)(2,1)S(1)}, bf16[8,4096]{1,0:T(8,128)(2,1)S(1)}, u32[]{:S(2)}, u32[]{:S(2)}) %collective-permute-start.3) | collective-permute-done | bytes 65568 | tf_op jit(solution)/shard_map/ppermute | solution.py:66
  51.4 0.7 pad_maximum_fusion
  52.1 1.9 %collective-permute-start.4 = (bf16[8,8192]{1,0:T(8,128)(2,1)S(1)}, bf16[8,8192]{1,0:T(8,128)(2,1)S(1)}, u32[]{:S(2)}, u32[]{:S(2)}) collective-permute-start(bf16[8,8192]{1,0:T(8,128)(2,1)S(1)} %pad_maximum_fusion), channel_id=1, source_target_pairs={{0,1},{1,0},{2,3},{3,2},{4,5},{5,4},{6,7},{7,6},{8,9},{9,8},{10,11... | collective-permute-start | bytes 393224 | tf_op jit(solution)/shard_map/ppermute | solution.py:66
  54.1 1.3 collective-permute-done.4
  55.4 0.0 copy-start.1
  55.4 0.0 collective-permute-done.far_index
  55.4 0.0 copy-start.3
  55.4 0.7 copy-done.1
  56.1 0.0 copy-done.3
  56.1 1.9 %shard_map.46 = (bf16[16,8,256]{2,1,0:T(8,128)(2,1)}, bf16[16,8,256]{2,1,0:T(8,128)(2,1)}) custom-call(s32[16]{0:T(128)} %get-tuple-element.10.near_index, s32[16]{0:T(128)} %copy-done.3, s32[1]{0:T(128)} %bitcast.2.own_ref, bf16[8,16384]{1,0:T(8,128)(2,1)} %copy-done.1), custom_call_target="tpu_custom_call" | custom-call | tf_op jit(solution)/shard_map/pallas_call | solution.py:71
  58.0 1.5 %collective-permute-start.5 = (bf16[16,8,256]{2,1,0:T(8,128)(2,1)}, bf16[16,8,256]{2,1,0:T(8,128)(2,1)S(1)}, u32[]{:S(2)}, u32[]{:S(2)}) collective-permute-start(bf16[16,8,256]{2,1,0:T(8,128)(2,1)} %get-tuple-element.7), channel_id=1, source_target_pairs={{0,0},{17,1},{34,2},{51,3},{68,4},{85,5},{102,6},{119,7},{136,8},{... | collective-permute-start | bytes 196616 | tf_op jit(solution)/shard_map/ppermute | solution.py:77
  59.5 0.0 copy-done
  59.5 1.5 %fusion.4 = f32[16,8,256]{2,1,0:T(8,128)S(1)} fusion(bf16[16,8,256]{2,1,0:T(8,128)(2,1)} %get-tuple-element.8, bf16[1,1,16,256,256]{4,3,2,1,0:T(8,128)(2,1)S(1)} %copy-done, pred[16]{0:T(512)(128)(4,1)S(1)} %iota_compare_fusion), kind=kOutput, calls=%fused_computation.4 | convolution fusion | flops 16809984 | bytes 2293776 | tf_op jit(solution)/shard_map/kva,kba->kvb/dot_general | solution.py:79
  61.0 0.7 collective-permute-start.6
  61.7 0.0 collective-permute-done.5
  61.7 1.1 fusion.2.trans
  62.7 0.0 collective-permute-done.6.arrived
  62.7 0.0 copy-start.2
  62.7 0.7 copy-done.2
  63.4 2.1 %shard_map.47 = f32[8,16384]{1,0:T(8,128)} custom-call(s32[16]{0:T(128)} %get-tuple-element.10.near_index, s32[16]{0:T(128)} %copy-done.3, s32[1]{0:T(128)} %bitcast.2.own_ref, s32[1]{0:T(128)} %bitcast.4.count_ref, f32[16,8,256]{2,1,0:T(8,128)} %fusion.2.trans, f32[16,8,256]{2,1,0:T(8,128)} %copy-done.2), custom_call_target="tpu_custom_call" | custom-call | tf_op jit(solution)/shard_map/pallas_call | solution.py:84
  65.5 1.0 slice.41
  66.5 9.5 %collective-permute-start.7 = (f32[8,8192]{1,0:T(8,128)S(1)}, f32[8,8192]{1,0:T(8,128)S(1)}, u32[]{:S(2)}, u32[]{:S(2)}) collective-permute-start(f32[8,8192]{1,0:T(8,128)S(1)} %slice.41), channel_id=1, source_target_pairs={{0,1},{1,0},{2,3},{3,2},{4,5},{5,4},{6,7},{7,6},{8,9},{9,8},{10,11... | collective-permute-start | bytes 786440 | tf_op jit(solution)/shard_map/ppermute | solution.py:93
  76.0 1.1 collective-permute-done.7
  77.2 1.0 slice_add_fusion
  78.2 20.6 %collective-permute-start.8 = (f32[8,4096]{1,0:T(8,128)S(1)}, f32[8,4096]{1,0:T(8,128)S(1)}, u32[]{:S(2)}, u32[]{:S(2)}) collective-permute-start(f32[8,4096]{1,0:T(8,128)S(1)} %slice.43), channel_id=1, source_target_pairs={{0,2},{1,3},{2,0},{3,1},{4,6},{5,7},{6,4},{7,5},{8,10},{9,11},{10,... | collective-permute-start | bytes 393224 | tf_op jit(solution)/shard_map/ppermute | solution.py:93
  98.8 4.0 %collective-permute-done.8 = f32[8,4096]{1,0:T(8,128)S(1)} collective-permute-done((f32[8,4096]{1,0:T(8,128)S(1)}, f32[8,4096]{1,0:T(8,128)S(1)}, u32[]{:S(2)}, u32[]{:S(2)}) %collective-permute-start.8) | collective-permute-done | bytes 131104 | tf_op jit(solution)/shard_map/ppermute | solution.py:93
  102.9 15.0 %collective-permute-start.9 = (f32[8,2048]{1,0:T(8,128)S(1)}, f32[8,2048]{1,0:T(8,128)S(1)}, u32[]{:S(2)}, u32[]{:S(2)}) collective-permute-start(f32[8,2048]{1,0:T(8,128)S(1)} %slice.45), channel_id=1, source_target_pairs={{0,4},{1,5},{2,6},{3,7},{4,0},{5,1},{6,2},{7,3},{8,12},{9,13},{10,... | collective-permute-start | bytes 196616 | tf_op jit(solution)/shard_map/ppermute | solution.py:93
  117.9 2.7 %collective-permute-done.9 = f32[8,2048]{1,0:T(8,128)S(1)} collective-permute-done((f32[8,2048]{1,0:T(8,128)S(1)}, f32[8,2048]{1,0:T(8,128)S(1)}, u32[]{:S(2)}, u32[]{:S(2)}) %collective-permute-start.9) | collective-permute-done | bytes 65568 | tf_op jit(solution)/shard_map/ppermute | solution.py:93
  120.7 4.7 %collective-permute-start.10 = (f32[8,1024]{1,0:T(8,128)S(1)}, f32[8,1024]{1,0:T(8,128)S(1)}, u32[]{:S(2)}, u32[]{:S(2)}) collective-permute-start(f32[8,1024]{1,0:T(8,128)S(1)} %slice.47), channel_id=1, source_target_pairs={{0,8},{1,9},{2,10},{3,11},{4,12},{5,13},{6,14},{7,15},{8,0},{9,1},... | collective-permute-start | bytes 98312 | tf_op jit(solution)/shard_map/ppermute | solution.py:93
  125.4 5.0 %collective-permute-done.10 = f32[8,1024]{1,0:T(8,128)S(1)} collective-permute-done((f32[8,1024]{1,0:T(8,128)S(1)}, f32[8,1024]{1,0:T(8,128)S(1)}, u32[]{:S(2)}, u32[]{:S(2)}) %collective-permute-start.10) | collective-permute-done | bytes 32800 | tf_op jit(solution)/shard_map/ppermute | solution.py:93
  130.4 0.6 slice_add_fusion.3
  (10 shorter events, 0.1 us)
Async XLA Ops:
  0.0 59.5 %copy-start = (bf16[1,1,16,256,256]{4,3,2,1,0:T(8,128)(2,1)S(1)}, bf16[1,1,16,256,256]{4,3,2,1,0:T(8,128)(2,1)}, u32[]{:S(2)}) copy-start(bf16[1,1,16,256,256]{4,3,2,1,0:T(8,128)(2,1)} %param.5) | copy-start | bytes 6291460
  1.4 54.0 %collective-permute-start = (s32[16]{0:T(128)S(1)}, s32[16]{0:T(128)S(1)}, u32[]{:S(2)}, u32[]{:S(2)}) collective-permute-start(s32[16]{0:T(128)S(1)} %get-tuple-element.9), channel_id=1, source_target_pairs={{0,0},{1,17},{2,34},{3,51},{4,68},{5,85},{6,102},{7,119},{8,136},{... | collective-permute-start | bytes 200 | tf_op jit(solution)/shard_map/ppermute | solution.py:62
  2.0 34.5 %collective-permute-start.1 = (bf16[8,1024]{1,0:T(8,128)(2,1)}, bf16[8,1024]{1,0:T(8,128)(2,1)S(1)}, u32[]{:S(2)}, u32[]{:S(2)}) collective-permute-start(bf16[8,1024]{1,0:T(8,128)(2,1)} %param.4), channel_id=1, source_target_pairs={{0,8},{1,9},{2,10},{3,11},{4,12},{5,13},{6,14},{7,15},{8,0},{9,1},... | collective-permute-start | bytes 49160 | tf_op jit(solution)/shard_map/ppermute | solution.py:66
  37.3 7.0 %collective-permute-start.2 = (bf16[8,2048]{1,0:T(8,128)(2,1)S(1)}, bf16[8,2048]{1,0:T(8,128)(2,1)S(1)}, u32[]{:S(2)}, u32[]{:S(2)}) collective-permute-start(bf16[8,2048]{1,0:T(8,128)(2,1)S(1)} %pad_maximum_fusion.2), channel_id=1, source_target_pairs={{0,4},{1,5},{2,6},{3,7},{4,0},{5,1},{6,2},{7,3},{8,12},{9,13},{10,... | collective-permute-start | bytes 98312 | tf_op jit(solution)/shard_map/ppermute | solution.py:66
  45.0 6.4 %collective-permute-start.3 = (bf16[8,4096]{1,0:T(8,128)(2,1)S(1)}, bf16[8,4096]{1,0:T(8,128)(2,1)S(1)}, u32[]{:S(2)}, u32[]{:S(2)}) collective-permute-start(bf16[8,4096]{1,0:T(8,128)(2,1)S(1)} %pad_maximum_fusion.1), channel_id=1, source_target_pairs={{0,2},{1,3},{2,0},{3,1},{4,6},{5,7},{6,4},{7,5},{8,10},{9,11},{10,... | collective-permute-start | bytes 196616 | tf_op jit(solution)/shard_map/ppermute | solution.py:66
  52.1 3.2 %collective-permute-start.4 = (bf16[8,8192]{1,0:T(8,128)(2,1)S(1)}, bf16[8,8192]{1,0:T(8,128)(2,1)S(1)}, u32[]{:S(2)}, u32[]{:S(2)}) collective-permute-start(bf16[8,8192]{1,0:T(8,128)(2,1)S(1)} %pad_maximum_fusion), channel_id=1, source_target_pairs={{0,1},{1,0},{2,3},{3,2},{4,5},{5,4},{6,7},{7,6},{8,9},{9,8},{10,11... | collective-permute-start | bytes 393224 | tf_op jit(solution)/shard_map/ppermute | solution.py:66
  55.4 0.7 copy-start.1
  55.4 0.7 copy-start.3
  58.0 3.7 %collective-permute-start.5 = (bf16[16,8,256]{2,1,0:T(8,128)(2,1)}, bf16[16,8,256]{2,1,0:T(8,128)(2,1)S(1)}, u32[]{:S(2)}, u32[]{:S(2)}) collective-permute-start(bf16[16,8,256]{2,1,0:T(8,128)(2,1)} %get-tuple-element.7), channel_id=1, source_target_pairs={{0,0},{17,1},{34,2},{51,3},{68,4},{85,5},{102,6},{119,7},{136,8},{... | collective-permute-start | bytes 196616 | tf_op jit(solution)/shard_map/ppermute | solution.py:77
  61.0 1.7 %collective-permute-start.6 = (f32[16,8,256]{2,1,0:T(8,128)S(1)}, f32[16,8,256]{2,1,0:T(8,128)S(1)}, u32[]{:S(2)}, u32[]{:S(2)}) collective-permute-start(f32[16,8,256]{2,1,0:T(8,128)S(1)} %fusion.4), channel_id=1, source_target_pairs={{0,0},{1,17},{2,34},{3,51},{4,68},{5,85},{6,102},{7,119},{8,136},{... | collective-permute-start | bytes 393224 | tf_op jit(solution)/shard_map/ppermute | solution.py:81
  62.7 0.7 copy-start.2
  66.5 10.7 %collective-permute-start.7 = (f32[8,8192]{1,0:T(8,128)S(1)}, f32[8,8192]{1,0:T(8,128)S(1)}, u32[]{:S(2)}, u32[]{:S(2)}) collective-permute-start(f32[8,8192]{1,0:T(8,128)S(1)} %slice.41), channel_id=1, source_target_pairs={{0,1},{1,0},{2,3},{3,2},{4,5},{5,4},{6,7},{7,6},{8,9},{9,8},{10,11... | collective-permute-start | bytes 786440 | tf_op jit(solution)/shard_map/ppermute | solution.py:93
  78.2 24.7 %collective-permute-start.8 = (f32[8,4096]{1,0:T(8,128)S(1)}, f32[8,4096]{1,0:T(8,128)S(1)}, u32[]{:S(2)}, u32[]{:S(2)}) collective-permute-start(f32[8,4096]{1,0:T(8,128)S(1)} %slice.43), channel_id=1, source_target_pairs={{0,2},{1,3},{2,0},{3,1},{4,6},{5,7},{6,4},{7,5},{8,10},{9,11},{10,... | collective-permute-start | bytes 393224 | tf_op jit(solution)/shard_map/ppermute | solution.py:93
  102.9 17.8 %collective-permute-start.9 = (f32[8,2048]{1,0:T(8,128)S(1)}, f32[8,2048]{1,0:T(8,128)S(1)}, u32[]{:S(2)}, u32[]{:S(2)}) collective-permute-start(f32[8,2048]{1,0:T(8,128)S(1)} %slice.45), channel_id=1, source_target_pairs={{0,4},{1,5},{2,6},{3,7},{4,0},{5,1},{6,2},{7,3},{8,12},{9,13},{10,... | collective-permute-start | bytes 196616 | tf_op jit(solution)/shard_map/ppermute | solution.py:93
  120.7 9.7 %collective-permute-start.10 = (f32[8,1024]{1,0:T(8,128)S(1)}, f32[8,1024]{1,0:T(8,128)S(1)}, u32[]{:S(2)}, u32[]{:S(2)}) collective-permute-start(f32[8,1024]{1,0:T(8,128)S(1)} %slice.47), channel_id=1, source_target_pairs={{0,8},{1,9},{2,10},{3,11},{4,12},{5,13},{6,14},{7,15},{8,0},{9,1},... | collective-permute-start | bytes 98312 | tf_op jit(solution)/shard_map/ppermute | solution.py:93

commit v2 on v1

v2 whole, which is shorter than its diff:
```python
import jax
import jax.numpy as jnp
from jax import lax
from jax.experimental import pallas as pl
from jax.experimental.pallas import tpu as pltpu
from jax.sharding import PartitionSpec as P

SERVER = (
    (4, 5, 3, 2, 9, 0, 1, 14, 15, 12, 11, 10, 13, 8, 6, 7),
    (7, 1, 2, 4, 5, 6, 0, 3, 15, 14, 11, 13, 8, 10, 9, 12),
    (5, 2, 9, 6, 4, 7, 1, 15, 14, 0, 3, 8, 10, 12, 13, 11),
    (2, 0, 6, 4, 7, 8, 5, 9, 12, 14, 1, 3, 15, 11, 10, 13),
)
SMEM = pl.BlockSpec(memory_space=pltpu.SMEM)
VMEM = pl.BlockSpec(memory_space=pltpu.VMEM)


def block_slice(block, width, per_piece):
    return pl.ds(pl.multiple_of(block % per_piece * width, width), width)


def pick_kernel(index, segment, rows):
    slots, _, width = rows.shape
    per_piece = segment.shape[-1] // width
    for slot in range(slots):
        block = index[slot]
        rows[slot] = segment[block // per_piece, :, block_slice(block, width, per_piece)]


def place_first_kernel(index, own_ref, rows, total):
    slots, _, width = rows.shape
    per_piece = total.shape[-1] // width
    own = own_ref[0]
    total[...] = jnp.zeros_like(total)
    for slot in range(slots):
        block = index[slot]
        piece = block // per_piece
        total[(piece ^ own) & 1, piece // 2, :, block_slice(block, width, per_piece)] += rows[slot]


def place_second_kernel(index, own_ref, count_ref, rows, earlier, keep, send, total):
    slots, _, width = rows.shape
    per_piece = total.shape[-1] // width
    own = own_ref[0]
    count = count_ref[0]
    total[...] = earlier[...]
    for slot in range(slots):
        block = index[slot]
        piece = block // per_piece
        value = jnp.where(slot < count, rows[slot], 0.0)
        total[(piece ^ own) & 1, piece // 2, :, block_slice(block, width, per_piece)] += value
    send[...] = total[1]
    keep[...] = total[0]


def body(vectors, tile_blocks, block_pairs, tile_counts):
    row_count = lax.axis_size("row")
    col_count = lax.axis_size("col")
    col_index = lax.axis_index("col")
    row_index = lax.axis_index("row")
    blocks = tile_blocks[0, 0]
    pair_rows = block_pairs[0, 0, :, 0]
    pair_cols = block_pairs[0, 0, :, 1]
    slots, width, _ = blocks.shape
    vec_count, piece = vectors.shape
    half_count = col_count // 2
    own = col_index.astype(jnp.int32)[None]
    in_band = row_index + col_index < row_count
    count = jnp.where(in_band, tile_counts[0, 0], 0)
    live = (jnp.arange(slots) < count)[:, None, None]
    both = ("row", "col")
    up = [(r * col_count + c, (r + c) * col_count + SERVER[(r + c) % 4][c])
          for r in range(row_count) for c in range(col_count) if r + c < row_count]
    down = [(b, a) for a, b in up]

    far_index = lax.ppermute(jnp.broadcast_to(pair_rows, (16, slots)), both, up)[0]
    copies = jnp.broadcast_to(vectors, (col_count, vec_count, piece))
    segment = lax.all_to_all(copies, "col", 0, 0, tiled=True)

    cost = pl.CostEstimate(flops=0, bytes_accessed=1000000, transcendentals=0)
    rows_type = jax.ShapeDtypeStruct((slots, vec_count, width), vectors.dtype)
    pick = pl.pallas_call(
        pick_kernel, out_shape=rows_type, in_specs=[SMEM, VMEM], out_specs=VMEM, cost_estimate=cost,
    )
    normal = jnp.einsum("kva,kba->kvb", pick(pair_cols, segment), blocks, preferred_element_type=jnp.float32)
    normal = jnp.where(live, normal, 0.0)
    arrived = lax.ppermute(normal, both, up)
    late_index, _ = lax.optimization_barrier((far_index, normal))
    far_rows = lax.ppermute(pick(late_index, segment), both, down)

    halves = (2, half_count, vec_count, piece)
    normal_total = pl.pallas_call(
        place_first_kernel,
        out_shape=jax.ShapeDtypeStruct(halves, jnp.float32),
        in_specs=[SMEM, SMEM, VMEM], out_specs=VMEM, cost_estimate=cost,
    )(far_index, own, arrived)
    far_rows, normal_total = lax.optimization_barrier((far_rows, normal_total))
    trans = jnp.einsum("kvb,kba->kva", far_rows, blocks, preferred_element_type=jnp.float32)
    half_type = jax.ShapeDtypeStruct(halves[1:], jnp.float32)
    keep, send = pl.pallas_call(
        place_second_kernel,
        out_shape=(half_type, half_type),
        in_specs=[SMEM, SMEM, SMEM, VMEM, VMEM], out_specs=(VMEM, VMEM),
        scratch_shapes=[pltpu.VMEM(halves, jnp.float32)], cost_estimate=cost,
    )(pair_cols, own, count[None], trans, normal_total)

    swap = [(c, c ^ 1) for c in range(col_count)]
    groups = [list(range(core, col_count, 2)) for core in range(2)]
    total = keep + lax.ppermute(send, "col", swap)
    parts = lax.all_to_all(total, "col", 0, 0, axis_index_groups=groups, tiled=True)
    return jnp.sum(parts, axis=0)


def solution(mesh):
    in_specs = (
        P(None, ("row", "col")),
        P("row", "col", None, None, None),
        P("row", "col", None, None),
        P("row", "col"),
    )
    out_specs = P(None, ("row", "col"))
    return jax.shard_map(body, mesh=mesh, in_specs=in_specs, out_specs=out_specs, check_vma=False)
```

time: 132 us -> 111 us (0.84)
  the two profiles are of different devices: /device:TPU:26 before, /device:TPU:8 now
where the time goes in v2:
time: 111 us
  starting transfers between devices  40.7 us (37%)
  blocking collectives  33 us (30%)
  waiting for transfers between devices  20.1 us (18%)
  Pallas kernels  7.49 us (7%)
  local copies, waits for them, and re-layouts  4.76 us (4%)
  matrix products  2.52 us (2%)
  other arithmetic  1.63 us (1%)
    all_to_all x1, blocking collectives, body(): lax.all_to_all(total, 'col', 0, 0, axis_index_groups=groups, tiled=True)  33 us
    all_to_all x1, starting transfers between devices, body(): segment = lax.all_to_all(copies, 'col', 0, 0, tiled=True)  12.6 us
    ppermute x1, starting transfers between devices, body(): far_rows = lax.ppermute(pick(late_index, segment), both, down)  11.4 us
    ppermute x1, starting transfers between devices, body(): arrived = lax.ppermute(normal, both, up)  10.1 us
    all_to_all x1, waiting for transfers between devices, body(): segment = lax.all_to_all(copies, 'col', 0, 0, tiled=True)  8.42 us
    ppermute x1, waiting for transfers between devices, body(): lax.ppermute(jnp.broadcast_to(pair_rows, (16, slots)), both, up)[0]  5.04 us
    ppermute x1, waiting for transfers between devices, body(): far_rows = lax.ppermute(pick(late_index, segment), both, down)  4.91 us
    ppermute x1, starting transfers between devices, body(): lax.ppermute(jnp.broadcast_to(pair_rows, (16, slots)), both, up)[0]  4.72 us
  transfers between devices with their start and end apart: 5, of which 4 were waited for; matrix products, arithmetic and copies ran while one was open for 3% of the time, Pallas kernels for 5%

profile of v2, /device:TPU:8, one launch (start us, length us, event | category | flops | bytes accessed | tf_op | source)
XLA Modules:
  0.0 111.0 jit_solution(8308660305686901461)
XLA Ops:
  0.0 0.0 copy-start
  0.0 1.6 %broadcast_in_dim.29 = bf16[16,8,1024]{2,1,0:T(8,128)(2,1)} broadcast(bf16[8,1024]{1,0:T(8,128)(2,1)} %param.4), dimensions={1,2} | broadcast | bytes 278528 | tf_op jit(solution)/shard_map/broadcast_in_dim | solution.py:77
  1.6 12.6 %all-to-all-start = ((bf16[16,8,1024]{2,1,0:T(8,128)(2,1)}), bf16[16,8,1024]{2,1,0:T(8,128)(2,1)S(1)}, u32[]{:S(2)}, u32[]{:S(2)}) async-start(bf16[16,8,1024]{2,1,0:T(8,128)(2,1)} %broadcast_in_dim.29), calls=%async_computation | async-start | bytes 524288 | tf_op jit(solution)/shard_map/all_to_all | solution.py:78
  14.2 1.3 %slice_bitcast_fusion.1 = (s32[16]{0:T(128)S(1)}, s32[16]{0:T(128)}) fusion(s32[1,1,16,2]{2,3,1,0:T(2,128)} %param.6), kind=kLoop, calls=%fused_computation.7 | loop fusion | bytes 256 | tf_op jit(solution)/shard_map/squeeze | solution.py:62
  15.5 4.7 %collective-permute-start = (s32[16,16]{1,0:T(8,128)S(1)}, s32[16,16]{1,0:T(8,128)S(1)}, u32[]{:S(2)}, u32[]{:S(2)}) collective-permute-start(s32[16,16]{1,0:T(8,128)S(1)} %broadcast_in_dim.27), channel_id=1, source_target_pairs={{0,4},{1,17},{2,41},{3,52},{4,73},{5,86},{6,97},{7,121},{8,143},{9... | collective-permute-start | bytes 3080 | tf_op jit(solution)/shard_map/ppermute | solution.py:76
  20.9 8.4 %all-to-all-done.segment = bf16[16,8,1024]{2,1,0:T(8,128)(2,1)S(1)} async-done(((bf16[16,8,1024]{2,1,0:T(8,128)(2,1)}), bf16[16,8,1024]{2,1,0:T(8,128)(2,1)S(1)}, u32[]{:S(2)}, u32[]{:S(2)}) %all-to-all-start) | async-done | bytes 262176 | tf_op jit(solution)/shard_map/all_to_all | solution.py:78
  29.3 0.0 copy-start.1
  29.3 0.7 copy-done.1
  30.0 1.7 %shard_map.46 = bf16[16,8,256]{2,1,0:T(8,128)(2,1)} custom-call(s32[16]{0:T(128)} %get-tuple-element.16.index, bf16[16,8,1024]{2,1,0:T(8,128)(2,1)} %copy-done.1), custom_call_target="tpu_custom_call" | custom-call | bytes 1000000 | tf_op jit(solution)/shard_map/pallas_call | solution.py:85
  31.7 0.0 copy-done
  31.7 1.5 %fusion.4 = f32[16,8,256]{2,1,0:T(8,128)S(1)} fusion(bf16[16,8,256]{2,1,0:T(8,128)(2,1)} %shard_map.46, bf16[1,1,16,256,256]{4,3,2,1,0:T(8,128)(2,1)S(1)} %copy-done, pred[16]{0:T(512)(128)(4,1)S(1)} %iota_compare_fusion), kind=kOutput, calls=%fused_computation.4 | convolution fusion | flops 16809984 | bytes 2293776 | tf_op jit(solution)/shard_map/kva,kba->kvb/dot_general | solution.py:85
  33.2 10.1 %collective-permute-start.2 = (f32[16,8,256]{2,1,0:T(8,128)S(1)}, f32[16,8,256]{2,1,0:T(8,128)S(1)}, u32[]{:S(2)}, u32[]{:S(2)}) collective-permute-start(f32[16,8,256]{2,1,0:T(8,128)S(1)} %fusion.4), channel_id=1, source_target_pairs={{0,4},{1,17},{2,41},{3,52},{4,73},{5,86},{6,97},{7,121},{8,143},{9... | collective-permute-start | bytes 393224 | tf_op jit(solution)/shard_map/ppermute | solution.py:87
  43.3 5.0 %collective-permute-done = s32[16,16]{1,0:T(8,128)S(1)} collective-permute-done((s32[16,16]{1,0:T(8,128)S(1)}, s32[16,16]{1,0:T(8,128)S(1)}, u32[]{:S(2)}, u32[]{:S(2)}) %collective-permute-start) | collective-permute-done | bytes 1056 | tf_op jit(solution)/shard_map/ppermute | solution.py:76
  48.3 0.6 slice_bitcast_fusion.index
  48.9 1.7 %shard_map.47 = bf16[16,8,256]{2,1,0:T(8,128)(2,1)} custom-call(s32[16]{0:T(128)} %slice_bitcast_fusion.index, bf16[16,8,1024]{2,1,0:T(8,128)(2,1)} %copy-done.1), custom_call_target="tpu_custom_call" | custom-call | bytes 1000000 | tf_op jit(solution)/shard_map/pallas_call | solution.py:89
  50.6 11.4 %collective-permute-start.1 = (bf16[16,8,256]{2,1,0:T(8,128)(2,1)}, bf16[16,8,256]{2,1,0:T(8,128)(2,1)S(1)}, u32[]{:S(2)}, u32[]{:S(2)}) collective-permute-start(bf16[16,8,256]{2,1,0:T(8,128)(2,1)} %shard_map.47), channel_id=1, source_target_pairs={{4,0},{17,1},{41,2},{52,3},{73,4},{86,5},{97,6},{121,7},{143,8},{1... | collective-permute-start | bytes 196616 | tf_op jit(solution)/shard_map/ppermute | solution.py:89
  62.0 0.0 collective-permute-done.2.rows
  62.0 0.0 copy-start.2
  62.0 0.6 copy-done.2
  62.6 1.9 %shard_map.48.earlier = f32[2,8,8,1024]{3,2,1,0:T(8,128)} custom-call(s32[16]{0:T(128)} %slice_bitcast_fusion.index, s32[1]{0:T(128)} %bitcast.1.own_ref, f32[16,8,256]{2,1,0:T(8,128)} %copy-done.2), custom_call_target="tpu_custom_call" | custom-call | bytes 1000000 | tf_op jit(solution)/shard_map/pallas_call | solution.py:92
  64.5 4.9 %collective-permute-done.1 = bf16[16,8,256]{2,1,0:T(8,128)(2,1)S(1)} collective-permute-done((bf16[16,8,256]{2,1,0:T(8,128)(2,1)}, bf16[16,8,256]{2,1,0:T(8,128)(2,1)S(1)}, u32[]{:S(2)}, u32[]{:S(2)}) %collective-permute-start.1) | collective-permute-done | bytes 65568 | tf_op jit(solution)/shard_map/ppermute | solution.py:89
  69.5 1.0 fusion.rows
  70.5 2.2 %shard_map.49 = (f32[8,8,1024]{2,1,0:T(8,128)}, f32[8,8,1024]{2,1,0:T(8,128)}) custom-call(s32[16]{0:T(128)} %get-tuple-element.16.index, s32[1]{0:T(128)} %bitcast.1.own_ref, s32[1]{0:T(128)} %bitcast.3.count_ref, f32[16,8,256]{2,1,0:T(8,128)} %fusion.rows, f32[2,8,8,1024]{3,2,1,0:T(8,128)} %shard_map.48.earlier), custom_call_target="tpu_custom_call" | custom-call | bytes 1000000 | tf_op jit(solution)/shard_map/pallas_call | solution.py:100
  72.7 1.9 %collective-permute-start.3 = (f32[8,8,1024]{2,1,0:T(8,128)}, f32[8,8,1024]{2,1,0:T(8,128)S(1)}, u32[]{:S(2)}, u32[]{:S(2)}) collective-permute-start(f32[8,8,1024]{2,1,0:T(8,128)} %get-tuple-element.14), channel_id=1, source_target_pairs={{0,1},{1,0},{2,3},{3,2},{4,5},{5,4},{6,7},{7,6},{8,9},{9,8},{10,11... | collective-permute-start | bytes 786440 | tf_op jit(solution)/shard_map/ppermute | solution.py:109
  74.6 1.7 %collective-permute-done.3 = f32[8,8,1024]{2,1,0:T(8,128)S(1)} collective-permute-done((f32[8,8,1024]{2,1,0:T(8,128)}, f32[8,8,1024]{2,1,0:T(8,128)S(1)}, u32[]{:S(2)}, u32[]{:S(2)}) %collective-permute-start.3) | collective-permute-done | bytes 262176 | tf_op jit(solution)/shard_map/ppermute | solution.py:109
  76.3 1.0 add.7
  77.3 33.0 %all_to_all.10 = f32[8,8,1024]{2,1,0:T(8,128)S(1)} all-to-all(f32[8,8,1024]{2,1,0:T(8,128)S(1)} %add.7), channel_id=1, replica_groups={{0,2,4,6,8,10,12,14},{1,3,5,7,9,11,13,15},{16,18,20,22,24,26,28,30},{17..., dimensions={0} | all-to-all | bytes 524288 | tf_op jit(solution)/shard_map/all_to_all | solution.py:110
  110.3 0.6 reduce_sum.9
  (2 shorter events, 0.0 us)
Async XLA Ops:
  0.0 31.7 %copy-start = (bf16[1,1,16,256,256]{4,3,2,1,0:T(8,128)(2,1)S(1)}, bf16[1,1,16,256,256]{4,3,2,1,0:T(8,128)(2,1)}, u32[]{:S(2)}) copy-start(bf16[1,1,16,256,256]{4,3,2,1,0:T(8,128)(2,1)} %param.5) | copy-start | bytes 6291460
  1.6 27.7 %all-to-all-start = ((bf16[16,8,1024]{2,1,0:T(8,128)(2,1)}), bf16[16,8,1024]{2,1,0:T(8,128)(2,1)S(1)}, u32[]{:S(2)}, u32[]{:S(2)}) async-start(bf16[16,8,1024]{2,1,0:T(8,128)(2,1)} %broadcast_in_dim.29), calls=%async_computation | async-start | bytes 524288 | tf_op jit(solution)/shard_map/all_to_all | solution.py:78
  15.5 32.8 %collective-permute-start = (s32[16,16]{1,0:T(8,128)S(1)}, s32[16,16]{1,0:T(8,128)S(1)}, u32[]{:S(2)}, u32[]{:S(2)}) collective-permute-start(s32[16,16]{1,0:T(8,128)S(1)} %broadcast_in_dim.27), channel_id=1, source_target_pairs={{0,4},{1,17},{2,41},{3,52},{4,73},{5,86},{6,97},{7,121},{8,143},{9... | collective-permute-start | bytes 3080 | tf_op jit(solution)/shard_map/ppermute | solution.py:76
  29.3 0.7 copy-start.1
  33.2 28.8 %collective-permute-start.2 = (f32[16,8,256]{2,1,0:T(8,128)S(1)}, f32[16,8,256]{2,1,0:T(8,128)S(1)}, u32[]{:S(2)}, u32[]{:S(2)}) collective-permute-start(f32[16,8,256]{2,1,0:T(8,128)S(1)} %fusion.4), channel_id=1, source_target_pairs={{0,4},{1,17},{2,41},{3,52},{4,73},{5,86},{6,97},{7,121},{8,143},{9... | collective-permute-start | bytes 393224 | tf_op jit(solution)/shard_map/ppermute | solution.py:87
  50.6 18.9 %collective-permute-start.1 = (bf16[16,8,256]{2,1,0:T(8,128)(2,1)}, bf16[16,8,256]{2,1,0:T(8,128)(2,1)S(1)}, u32[]{:S(2)}, u32[]{:S(2)}) collective-permute-start(bf16[16,8,256]{2,1,0:T(8,128)(2,1)} %shard_map.47), channel_id=1, source_target_pairs={{4,0},{17,1},{41,2},{52,3},{73,4},{86,5},{97,6},{121,7},{143,8},{1... | collective-permute-start | bytes 196616 | tf_op jit(solution)/shard_map/ppermute | solution.py:89
  62.0 0.7 copy-start.2
  72.7 3.6 %collective-permute-start.3 = (f32[8,8,1024]{2,1,0:T(8,128)}, f32[8,8,1024]{2,1,0:T(8,128)S(1)}, u32[]{:S(2)}, u32[]{:S(2)}) collective-permute-start(f32[8,8,1024]{2,1,0:T(8,128)} %get-tuple-element.14), channel_id=1, source_target_pairs={{0,1},{1,0},{2,3},{3,2},{4,5},{5,4},{6,7},{7,6},{8,9},{9,8},{10,11... | collective-permute-start | bytes 786440 | tf_op jit(solution)/shard_map/ppermute | solution.py:109

commit v3 on v2

v3 whole, which is shorter than its diff:
```python
import jax
import jax.numpy as jnp
from jax import lax
from jax.experimental import pallas as pl
from jax.experimental.pallas import tpu as pltpu
from jax.sharding import PartitionSpec as P

SERVER = (
    (4, 5, 3, 2, 9, 0, 1, 14, 15, 12, 11, 10, 13, 8, 6, 7),
    (7, 1, 2, 4, 5, 6, 0, 3, 15, 14, 11, 13, 8, 10, 9, 12),
    (5, 2, 9, 6, 4, 7, 1, 15, 14, 0, 3, 8, 10, 12, 13, 11),
    (2, 0, 6, 4, 7, 8, 5, 9, 12, 14, 1, 3, 15, 11, 10, 13),
)
SMEM = pl.BlockSpec(memory_space=pltpu.SMEM)
VMEM = pl.BlockSpec(memory_space=pltpu.VMEM)


def in_vmem(array):
    return pltpu.with_memory_space_constraint(array, pltpu.VMEM)


def block_slice(block, width, per_piece):
    return pl.ds(pl.multiple_of(block % per_piece * width, width), width)


def pick_kernel(index, segment, rows):
    slots, _, width = rows.shape
    per_piece = segment.shape[-1] // width
    for slot in range(slots):
        block = index[slot]
        rows[slot] = segment[block // per_piece, :, block_slice(block, width, per_piece)]


def place_kernel(index, far_index, own_ref, count_ref, trans, arrived, late, keep, send, total):
    slots, _, width = trans.shape
    per_piece = total.shape[-1] // width
    own = own_ref[0]
    count = count_ref[0]
    total[...] = jnp.zeros_like(total)
    for slot in range(slots):
        product = jnp.where(slot < count, trans[slot], 0.0)
        for block, value in ((index[slot], product), (far_index[slot], arrived[slot] + late[slot])):
            piece = block // per_piece
            total[(piece ^ own) & 1, piece // 2, :, block_slice(block, width, per_piece)] += value
    send[...] = total[1]
    keep[...] = total[0]


def body(vectors, tile_blocks, block_pairs, tile_counts):
    row_count = lax.axis_size("row")
    col_count = lax.axis_size("col")
    col_index = lax.axis_index("col")
    row_index = lax.axis_index("row")
    blocks = tile_blocks[0, 0]
    pair_rows = block_pairs[0, 0, :, 0]
    pair_cols = block_pairs[0, 0, :, 1]
    slots, width, _ = blocks.shape
    vec_count, piece = vectors.shape
    half_count = col_count // 2
    own = col_index.astype(jnp.int32)[None]
    in_band = row_index + col_index < row_count
    count = jnp.where(in_band, tile_counts[0, 0], 0)
    live = (jnp.arange(slots) < count)[:, None, None]
    both = ("row", "col")
    up = [(r * col_count + c, (r + c) * col_count + SERVER[(r + c) % 4][c])
          for r in range(row_count) for c in range(col_count) if r + c < row_count]
    down = [(b, a) for a, b in up]

    def slack(tile, server):
        part = [device // col_count // 4 % 4 for device in (tile, server)]
        return part[1] == 2 or (part[0] == 0 and part[1] == 3)

    far_index = lax.ppermute(jnp.broadcast_to(pair_rows, (16, slots)), both, up)[0]
    copies = jnp.broadcast_to(vectors, (col_count, vec_count, piece))
    segment = lax.all_to_all(copies, "col", 0, 0, tiled=True)

    cost = pl.CostEstimate(flops=0, bytes_accessed=1000000, transcendentals=0)
    call = pl.pallas_call(
        pick_kernel, out_shape=pltpu.VMEM((slots, vec_count, width), vectors.dtype),
        in_specs=[SMEM, VMEM], out_specs=VMEM, cost_estimate=cost,
    )

    def pick(index):
        return call(index, in_vmem(segment))

    normal = jnp.einsum("kva,kba->kvb", pick(pair_cols), blocks, preferred_element_type=jnp.float32)
    normal = jnp.where(live, normal, 0.0)
    arrived = lax.ppermute(normal, both, [(a, b) for a, b in up if not slack(a, b)])
    late_index, _ = lax.optimization_barrier((far_index, normal))
    far_picked = pick(late_index)
    far_rows = lax.ppermute(far_picked, both, down)
    late_normal, _ = lax.optimization_barrier((normal, far_picked))
    late = lax.ppermute(late_normal, both, [(a, b) for a, b in up if slack(a, b)])

    halves = (2, half_count, vec_count, piece)
    far_rows, arrived = lax.optimization_barrier((far_rows, arrived))
    trans = jnp.einsum("kvb,kba->kva", far_rows, blocks, preferred_element_type=jnp.float32)
    half_type = pltpu.VMEM(halves[1:], jnp.float32)
    keep, send = pl.pallas_call(
        place_kernel,
        out_shape=(half_type, half_type),
        in_specs=[SMEM] * 4 + [VMEM] * 3, out_specs=(VMEM, VMEM),
        scratch_shapes=[pltpu.VMEM(halves, jnp.float32)], cost_estimate=cost,
    )(pair_cols, far_index, own, count[None], in_vmem(trans), in_vmem(arrived), in_vmem(late))

    swap = [(c, c ^ 1) for c in range(col_count)]
    groups = [list(range(core, col_count, 2)) for core in range(2)]
    total = keep + lax.ppermute(send, "col", swap)
    parts = lax.all_to_all(total, "col", 0, 0, axis_index_groups=groups, tiled=True)
    return jnp.sum(parts, axis=0)


def solution(mesh):
    in_specs = (
        P(None, ("row", "col")),
        P("row", "col", None, None, None),
        P("row", "col", None, None),
        P("row", "col"),
    )
    out_specs = P(None, ("row", "col"))
    return jax.shard_map(body, mesh=mesh, in_specs=in_specs, out_specs=out_specs, check_vma=False)
```

time: 111 us -> 104 us (0.937)
  the two profiles are of different devices: /device:TPU:8 before, /device:TPU:10 now
where the time goes in v3:
time: 104 us; the launch traced here: 103 us
  starting transfers between devices  41.1 us (40%)
  blocking collectives  38.9 us (37%)
  waiting for transfers between devices  14.8 us (14%)
  local copies, waits for them, and re-layouts  3.37 us (3%)
  Pallas kernels  2.68 us (3%)
    all_to_all x1, blocking collectives, body(): lax.all_to_all(total, 'col', 0, 0, axis_index_groups=groups, tiled=True)  38.9 us
    ppermute x1, starting transfers between devices, body(): lax.ppermute(normal, both, [(a, b) for a, b in up if not slack(a, b)])  13.6 us
    all_to_all x1, starting transfers between devices, body(): segment = lax.all_to_all(copies, 'col', 0, 0, tiled=True)  12.6 us
    all_to_all x1, waiting for transfers between devices, body(): segment = lax.all_to_all(copies, 'col', 0, 0, tiled=True)  7.86 us
    ppermute x1, starting transfers between devices, body(): far_rows = lax.ppermute(far_picked, both, down)  6.98 us
    ppermute x1, starting transfers between devices, body(): lax.ppermute(jnp.broadcast_to(pair_rows, (16, slots)), both, up)[0]  5.37 us
    ppermute x1, waiting for transfers between devices, body(): lax.ppermute(jnp.broadcast_to(pair_rows, (16, slots)), both, up)[0]  4.24 us
  transfers between devices with their start and end apart: 6, of which 4 were waited for; matrix products, arithmetic and copies ran while one was open for 3% of the time, Pallas kernels for 1%

profile of v3, /device:TPU:10, one launch (start us, length us, event | category | flops | bytes accessed | tf_op | source)
XLA Modules:
  0.0 103.4 jit_solution(9445867055606492617)
XLA Ops:
  0.0 0.0 copy-start
  0.0 1.6 %broadcast_in_dim.29 = bf16[16,8,1024]{2,1,0:T(8,128)(2,1)} broadcast(bf16[8,1024]{1,0:T(8,128)(2,1)} %param.4), dimensions={1,2} | broadcast | bytes 278528 | tf_op jit(solution)/shard_map/broadcast_in_dim | solution.py:74
  1.6 12.6 %all-to-all-start = ((bf16[16,8,1024]{2,1,0:T(8,128)(2,1)}), bf16[16,8,1024]{2,1,0:T(8,128)(2,1)S(1)}, u32[]{:S(2)}, u32[]{:S(2)}) async-start(bf16[16,8,1024]{2,1,0:T(8,128)(2,1)} %broadcast_in_dim.29), calls=%async_computation | async-start | bytes 524288 | tf_op jit(solution)/shard_map/all_to_all | solution.py:75
  14.2 1.3 %slice_bitcast_fusion.1 = (s32[16]{0:T(128)S(1)}, s32[16]{0:T(128)}) fusion(s32[1,1,16,2]{2,3,1,0:T(2,128)} %param.6), kind=kLoop, calls=%fused_computation.7 | loop fusion | bytes 256 | tf_op jit(solution)/shard_map/squeeze | solution.py:55
  15.5 5.4 %collective-permute-start = (s32[16,16]{1,0:T(8,128)S(1)}, s32[16,16]{1,0:T(8,128)S(1)}, u32[]{:S(2)}, u32[]{:S(2)}) collective-permute-start(s32[16,16]{1,0:T(8,128)S(1)} %broadcast_in_dim.25), channel_id=1, source_target_pairs={{0,4},{1,17},{2,41},{3,52},{4,73},{5,86},{6,97},{7,121},{8,143},{9... | collective-permute-start | bytes 3080 | tf_op jit(solution)/shard_map/ppermute | solution.py:73
  21.6 7.9 %all-to-all-done.segment = bf16[16,8,1024]{2,1,0:T(8,128)(2,1)S(1)} async-done(((bf16[16,8,1024]{2,1,0:T(8,128)(2,1)}), bf16[16,8,1024]{2,1,0:T(8,128)(2,1)S(1)}, u32[]{:S(2)}, u32[]{:S(2)}) %all-to-all-start) | async-done | bytes 262176 | tf_op jit(solution)/shard_map/all_to_all | solution.py:75
  29.4 0.8 shard_map.46
  30.2 0.0 copy-done
  30.2 0.6 fusion.4
  30.8 13.6 %collective-permute-start.2 = (f32[16,8,256]{2,1,0:T(8,128)S(1)}, f32[16,8,256]{2,1,0:T(8,128)S(1)}, u32[]{:S(2)}, u32[]{:S(2)}) collective-permute-start(f32[16,8,256]{2,1,0:T(8,128)S(1)} %fusion.4), channel_id=1, source_target_pairs={{0,4},{1,17},{2,41},{3,52},{4,73},{5,86},{6,97},{7,121},{16,23},{1... | collective-permute-start | bytes 393224 | tf_op jit(solution)/shard_map/ppermute | solution.py:88
  44.4 4.2 %collective-permute-done = s32[16,16]{1,0:T(8,128)S(1)} collective-permute-done((s32[16,16]{1,0:T(8,128)S(1)}, s32[16,16]{1,0:T(8,128)S(1)}, u32[]{:S(2)}, u32[]{:S(2)}) %collective-permute-start) | collective-permute-done | bytes 1056 | tf_op jit(solution)/shard_map/ppermute | solution.py:73
  48.7 0.5 slice_bitcast_fusion.index.far_index
  49.2 0.8 shard_map.47
  50.0 7.0 %collective-permute-start.1 = (bf16[16,8,256]{2,1,0:T(8,128)(2,1)S(1)}, bf16[16,8,256]{2,1,0:T(8,128)(2,1)S(1)}, u32[]{:S(2)}, u32[]{:S(2)}) collective-permute-start(bf16[16,8,256]{2,1,0:T(8,128)(2,1)S(1)} %shard_map.47), channel_id=1, source_target_pairs={{4,0},{17,1},{41,2},{52,3},{73,4},{86,5},{97,6},{121,7},{143,8},{1... | collective-permute-start | bytes 196616 | tf_op jit(solution)/shard_map/ppermute | solution.py:91
  56.9 0.7 collective-permute-start.3
  57.6 1.2 %collective-permute-done.1 = bf16[16,8,256]{2,1,0:T(8,128)(2,1)S(1)} collective-permute-done((bf16[16,8,256]{2,1,0:T(8,128)(2,1)S(1)}, bf16[16,8,256]{2,1,0:T(8,128)(2,1)S(1)}, u32[]{:S(2)}, u32[]{:S(2)}) %collective-permute-start.1) | collective-permute-done | bytes 65568 | tf_op jit(solution)/shard_map/ppermute | solution.py:91
  58.8 0.0 collective-permute-done.2.arrived
  58.8 0.4 fusion.trans
  59.2 0.0 collective-permute-done.3.late
  59.2 1.1 %shard_map.48 = (f32[8,8,1024]{2,1,0:T(8,128)S(1)}, f32[8,8,1024]{2,1,0:T(8,128)S(1)}) custom-call(s32[16]{0:T(128)} %get-tuple-element.18.index, s32[16]{0:T(128)} %slice_bitcast_fusion.index.far_index, s32[1]{0:T(128)} %bitcast.3.own_ref, s32[1]{0:T(128)} %bitcast.5.count_ref, f32[16,8,256]{2,1,0:T(8,128)S(1)} %fusion.trans, ...), custom_call_target="tpu_custom_call" | custom-call | bytes 1000000 | tf_op jit(solution)/shard_map/pallas_call | solution.py:99
  60.3 1.9 %collective-permute-start.4 = (f32[8,8,1024]{2,1,0:T(8,128)S(1)}, f32[8,8,1024]{2,1,0:T(8,128)S(1)}, u32[]{:S(2)}, u32[]{:S(2)}) collective-permute-start(f32[8,8,1024]{2,1,0:T(8,128)S(1)} %get-tuple-element.16), channel_id=1, source_target_pairs={{0,1},{1,0},{2,3},{3,2},{4,5},{5,4},{6,7},{7,6},{8,9},{9,8},{10,11... | collective-permute-start | bytes 786440 | tf_op jit(solution)/shard_map/ppermute | solution.py:108
  62.3 1.5 %collective-permute-done.4 = f32[8,8,1024]{2,1,0:T(8,128)S(1)} collective-permute-done((f32[8,8,1024]{2,1,0:T(8,128)S(1)}, f32[8,8,1024]{2,1,0:T(8,128)S(1)}, u32[]{:S(2)}, u32[]{:S(2)}) %collective-permute-start.4) | collective-permute-done | bytes 262176 | tf_op jit(solution)/shard_map/ppermute | solution.py:108
  63.8 38.9 %all_to_all.10 = f32[8,8,1024]{2,1,0:T(8,128)S(1)} all-to-all(f32[8,8,1024]{2,1,0:T(8,128)S(1)} %add.7), channel_id=1, replica_groups={{0,2,4,6,8,10,12,14},{1,3,5,7,9,11,13,15},{16,18,20,22,24,26,28,30},{17..., dimensions={0} | all-to-all | bytes 524288 | tf_op jit(solution)/shard_map/all_to_all | solution.py:109
  102.7 0.6 reduce_sum.9
  (3 shorter events, 0.1 us)
Async XLA Ops:
  0.0 30.2 %copy-start = (bf16[1,1,16,256,256]{4,3,2,1,0:T(8,128)(2,1)S(1)}, bf16[1,1,16,256,256]{4,3,2,1,0:T(8,128)(2,1)}, u32[]{:S(2)}) copy-start(bf16[1,1,16,256,256]{4,3,2,1,0:T(8,128)(2,1)} %param.5) | copy-start | bytes 6291460
  1.6 27.8 %all-to-all-start = ((bf16[16,8,1024]{2,1,0:T(8,128)(2,1)}), bf16[16,8,1024]{2,1,0:T(8,128)(2,1)S(1)}, u32[]{:S(2)}, u32[]{:S(2)}) async-start(bf16[16,8,1024]{2,1,0:T(8,128)(2,1)} %broadcast_in_dim.29), calls=%async_computation | async-start | bytes 524288 | tf_op jit(solution)/shard_map/all_to_all | solution.py:75
  15.5 33.2 %collective-permute-start = (s32[16,16]{1,0:T(8,128)S(1)}, s32[16,16]{1,0:T(8,128)S(1)}, u32[]{:S(2)}, u32[]{:S(2)}) collective-permute-start(s32[16,16]{1,0:T(8,128)S(1)} %broadcast_in_dim.25), channel_id=1, source_target_pairs={{0,4},{1,17},{2,41},{3,52},{4,73},{5,86},{6,97},{7,121},{8,143},{9... | collective-permute-start | bytes 3080 | tf_op jit(solution)/shard_map/ppermute | solution.py:73
  30.8 28.0 %collective-permute-start.2 = (f32[16,8,256]{2,1,0:T(8,128)S(1)}, f32[16,8,256]{2,1,0:T(8,128)S(1)}, u32[]{:S(2)}, u32[]{:S(2)}) collective-permute-start(f32[16,8,256]{2,1,0:T(8,128)S(1)} %fusion.4), channel_id=1, source_target_pairs={{0,4},{1,17},{2,41},{3,52},{4,73},{5,86},{6,97},{7,121},{16,23},{1... | collective-permute-start | bytes 393224 | tf_op jit(solution)/shard_map/ppermute | solution.py:88
  50.0 8.9 %collective-permute-start.1 = (bf16[16,8,256]{2,1,0:T(8,128)(2,1)S(1)}, bf16[16,8,256]{2,1,0:T(8,128)(2,1)S(1)}, u32[]{:S(2)}, u32[]{:S(2)}) collective-permute-start(bf16[16,8,256]{2,1,0:T(8,128)(2,1)S(1)} %shard_map.47), channel_id=1, source_target_pairs={{4,0},{17,1},{41,2},{52,3},{73,4},{86,5},{97,6},{121,7},{143,8},{1... | collective-permute-start | bytes 196616 | tf_op jit(solution)/shard_map/ppermute | solution.py:91
  56.9 2.3 %collective-permute-start.3 = (f32[16,8,256]{2,1,0:T(8,128)S(1)}, f32[16,8,256]{2,1,0:T(8,128)S(1)}, u32[]{:S(2)}, u32[]{:S(2)}) collective-permute-start(f32[16,8,256]{2,1,0:T(8,128)S(1)} %fusion.4), channel_id=1, source_target_pairs={{8,143},{9,158},{10,163},{11,179},{12,205},{13,218},{14,237},{15,2... | collective-permute-start | bytes 393224 | tf_op jit(solution)/shard_map/ppermute | solution.py:93
  60.3 3.4 %collective-permute-start.4 = (f32[8,8,1024]{2,1,0:T(8,128)S(1)}, f32[8,8,1024]{2,1,0:T(8,128)S(1)}, u32[]{:S(2)}, u32[]{:S(2)}) collective-permute-start(f32[8,8,1024]{2,1,0:T(8,128)S(1)} %get-tuple-element.16), channel_id=1, source_target_pairs={{0,1},{1,0},{2,3},{3,2},{4,5},{5,4},{6,7},{7,6},{8,9},{9,8},{10,11... | collective-permute-start | bytes 786440 | tf_op jit(solution)/shard_map/ppermute | solution.py:108

commit v4 on v3

--- a/solution.py
+++ b/solution.py
@@ -6,10 +6,10 @@
 from jax.sharding import PartitionSpec as P
 
 SERVER = (
-    (4, 5, 3, 2, 9, 0, 1, 14, 15, 12, 11, 10, 13, 8, 6, 7),
-    (7, 1, 2, 4, 5, 6, 0, 3, 15, 14, 11, 13, 8, 10, 9, 12),
-    (5, 2, 9, 6, 4, 7, 1, 15, 14, 0, 3, 8, 10, 12, 13, 11),
-    (2, 0, 6, 4, 7, 8, 5, 9, 12, 14, 1, 3, 15, 11, 10, 13),
+    (6, 5, 4, 7, 2, 14, 0, 1, 3, 12, 15, 10, 13, 11, 9, 8),
+    (2, 7, 3, 5, 4, 6, 1, 14, 15, 0, 13, 11, 12, 9, 8, 10),
+    (6, 3, 4, 5, 2, 7, 8, 15, 0, 14, 1, 11, 9, 10, 13, 12),
+    (8, 3, 7, 6, 9, 4, 5, 11, 0, 14, 1, 2, 10, 12, 13, 15),
 )
 SMEM = pl.BlockSpec(memory_space=pltpu.SMEM)
 VMEM = pl.BlockSpec(memory_space=pltpu.VMEM)

time: 104 us -> 103 us (level)
  waiting for transfers between devices: 14.8 us -> 20.2 us
  starting transfers between devices: 41.1 us -> 36.9 us
  blocking collectives: 38.9 us -> 37.2 us
    ppermute x1, starting transfers between devices: 13.6 us -> 3.04 us  [body(): lax.ppermute(normal, both, [(a, b) for a, b in up if not slack(a, b)])]
    ppermute x1, starting transfers between devices: 1.92 us -> 7.27 us  [body(): total = keep + lax.ppermute(send, 'col', swap)]
    ppermute x1, waiting for transfers between devices: 4.24 us -> 8.41 us  [body(): lax.ppermute(jnp.broadcast_to(pair_rows, (16, slots)), both, up)[0]]
    ppermute x1, starting transfers between devices: 6.98 us -> 9.45 us  [body(): far_rows = lax.ppermute(far_picked, both, down)]
    all_to_all x1, blocking collectives: 38.9 us -> 37.2 us  [body(): lax.all_to_all(total, 'col', 0, 0, axis_index_groups=groups, tiled=True)]
    all_to_all x1, waiting for transfers between devices: 7.86 us -> 9.41 us  [body(): segment = lax.all_to_all(copies, 'col', 0, 0, tiled=True)]
    ppermute x1, starting transfers between devices: 5.37 us -> 3.82 us  [body(): lax.ppermute(jnp.broadcast_to(pair_rows, (16, slots)), both, up)[0]]
  transfers between devices with their start and end apart: 6 -> 6, of which waited for: 4 -> 4; matrix products, arithmetic and copies ran while one was open for 3% -> 3% of each run, Pallas kernels for 1% -> 2%
where the time goes in v4:
time: 103 us
  blocking collectives  37.2 us (36%)
  starting transfers between devices  36.9 us (36%)
  waiting for transfers between devices  20.2 us (20%)
  local copies, waits for them, and re-layouts  3.37 us (3%)
  Pallas kernels  2.68 us (3%)
    all_to_all x1, blocking collectives, body(): lax.all_to_all(total, 'col', 0, 0, axis_index_groups=groups, tiled=True)  37.2 us
    all_to_all x1, starting transfers between devices, body(): segment = lax.all_to_all(copies, 'col', 0, 0, tiled=True)  12.6 us
    ppermute x1, starting transfers between devices, body(): far_rows = lax.ppermute(far_picked, both, down)  9.45 us
    all_to_all x1, waiting for transfers between devices, body(): segment = lax.all_to_all(copies, 'col', 0, 0, tiled=True)  9.41 us
    ppermute x1, waiting for transfers between devices, body(): lax.ppermute(jnp.broadcast_to(pair_rows, (16, slots)), both, up)[0]  8.41 us
    ppermute x1, starting transfers between devices, body(): total = keep + lax.ppermute(send, 'col', swap)  7.27 us
    ppermute x1, starting transfers between devices, body(): lax.ppermute(jnp.broadcast_to(pair_rows, (16, slots)), both, up)[0]  3.82 us
    ppermute x1, starting transfers between devices, body(): lax.ppermute(normal, both, [(a, b) for a, b in up if not slack(a, b)])  3.04 us
  transfers between devices with their start and end apart: 6, of which 4 were waited for; matrix products, arithmetic and copies ran while one was open for 3% of the time, Pallas kernels for 2%

profile of v4, /device:TPU:10, one launch (start us, length us, event | category | flops | bytes accessed | tf_op | source)
XLA Modules:
  0.0 102.8 jit_solution(10614817036445302793)
XLA Ops:
  0.0 0.0 copy-start
  0.0 1.6 %broadcast_in_dim.29 = bf16[16,8,1024]{2,1,0:T(8,128)(2,1)} broadcast(bf16[8,1024]{1,0:T(8,128)(2,1)} %param.4), dimensions={1,2} | broadcast | bytes 278528 | tf_op jit(solution)/shard_map/broadcast_in_dim | solution.py:74
  1.6 12.6 %all-to-all-start = ((bf16[16,8,1024]{2,1,0:T(8,128)(2,1)}), bf16[16,8,1024]{2,1,0:T(8,128)(2,1)S(1)}, u32[]{:S(2)}, u32[]{:S(2)}) async-start(bf16[16,8,1024]{2,1,0:T(8,128)(2,1)} %broadcast_in_dim.29), calls=%async_computation | async-start | bytes 524288 | tf_op jit(solution)/shard_map/all_to_all | solution.py:75
  14.2 1.3 %slice_bitcast_fusion.1 = (s32[16]{0:T(128)S(1)}, s32[16]{0:T(128)}) fusion(s32[1,1,16,2]{2,3,1,0:T(2,128)} %param.6), kind=kLoop, calls=%fused_computation.7 | loop fusion | bytes 256 | tf_op jit(solution)/shard_map/squeeze | solution.py:55
  15.5 3.8 %collective-permute-start = (s32[16,16]{1,0:T(8,128)S(1)}, s32[16,16]{1,0:T(8,128)S(1)}, u32[]{:S(2)}, u32[]{:S(2)}) collective-permute-start(s32[16,16]{1,0:T(8,128)S(1)} %broadcast_in_dim.25), channel_id=1, source_target_pairs={{0,6},{1,23},{2,36},{3,54},{4,66},{5,86},{6,104},{7,123},{8,131},{... | collective-permute-start | bytes 3080 | tf_op jit(solution)/shard_map/ppermute | solution.py:73
  20.0 9.4 %all-to-all-done.segment = bf16[16,8,1024]{2,1,0:T(8,128)(2,1)S(1)} async-done(((bf16[16,8,1024]{2,1,0:T(8,128)(2,1)}), bf16[16,8,1024]{2,1,0:T(8,128)(2,1)S(1)}, u32[]{:S(2)}, u32[]{:S(2)}) %all-to-all-start) | async-done | bytes 262176 | tf_op jit(solution)/shard_map/all_to_all | solution.py:75
  29.4 0.8 shard_map.46
  30.2 0.0 copy-done
  30.2 0.6 fusion.4
  30.8 3.0 %collective-permute-start.2 = (f32[16,8,256]{2,1,0:T(8,128)S(1)}, f32[16,8,256]{2,1,0:T(8,128)S(1)}, u32[]{:S(2)}, u32[]{:S(2)}) collective-permute-start(f32[16,8,256]{2,1,0:T(8,128)S(1)} %fusion.4), channel_id=1, source_target_pairs={{0,6},{1,23},{2,36},{3,54},{4,66},{5,86},{6,104},{7,123},{16,18},{... | collective-permute-start | bytes 393224 | tf_op jit(solution)/shard_map/ppermute | solution.py:88
  33.9 8.4 %collective-permute-done = s32[16,16]{1,0:T(8,128)S(1)} collective-permute-done((s32[16,16]{1,0:T(8,128)S(1)}, s32[16,16]{1,0:T(8,128)S(1)}, u32[]{:S(2)}, u32[]{:S(2)}) %collective-permute-start) | collective-permute-done | bytes 1056 | tf_op jit(solution)/shard_map/ppermute | solution.py:73
  42.3 0.5 slice_bitcast_fusion.index.far_index
  42.8 0.8 shard_map.47
  43.6 9.5 %collective-permute-start.1 = (bf16[16,8,256]{2,1,0:T(8,128)(2,1)S(1)}, bf16[16,8,256]{2,1,0:T(8,128)(2,1)S(1)}, u32[]{:S(2)}, u32[]{:S(2)}) collective-permute-start(bf16[16,8,256]{2,1,0:T(8,128)(2,1)S(1)} %shard_map.47), channel_id=1, source_target_pairs={{6,0},{23,1},{36,2},{54,3},{66,4},{86,5},{104,6},{123,7},{131,8},{... | collective-permute-start | bytes 196616 | tf_op jit(solution)/shard_map/ppermute | solution.py:91
  53.0 0.7 collective-permute-start.3
  53.7 1.2 %collective-permute-done.1 = bf16[16,8,256]{2,1,0:T(8,128)(2,1)S(1)} collective-permute-done((bf16[16,8,256]{2,1,0:T(8,128)(2,1)S(1)}, bf16[16,8,256]{2,1,0:T(8,128)(2,1)S(1)}, u32[]{:S(2)}, u32[]{:S(2)}) %collective-permute-start.1) | collective-permute-done | bytes 65568 | tf_op jit(solution)/shard_map/ppermute | solution.py:91
  54.9 0.0 collective-permute-done.2.arrived
  54.9 0.4 fusion.trans
  55.3 0.0 collective-permute-done.3.late
  55.3 1.1 %shard_map.48 = (f32[8,8,1024]{2,1,0:T(8,128)S(1)}, f32[8,8,1024]{2,1,0:T(8,128)S(1)}) custom-call(s32[16]{0:T(128)} %get-tuple-element.18.index, s32[16]{0:T(128)} %slice_bitcast_fusion.index.far_index, s32[1]{0:T(128)} %bitcast.3.own_ref, s32[1]{0:T(128)} %bitcast.5.count_ref, f32[16,8,256]{2,1,0:T(8,128)S(1)} %fusion.trans, ...), custom_call_target="tpu_custom_call" | custom-call | bytes 1000000 | tf_op jit(solution)/shard_map/pallas_call | solution.py:99
  56.5 7.3 %collective-permute-start.4 = (f32[8,8,1024]{2,1,0:T(8,128)S(1)}, f32[8,8,1024]{2,1,0:T(8,128)S(1)}, u32[]{:S(2)}, u32[]{:S(2)}) collective-permute-start(f32[8,8,1024]{2,1,0:T(8,128)S(1)} %get-tuple-element.16), channel_id=1, source_target_pairs={{0,1},{1,0},{2,3},{3,2},{4,5},{5,4},{6,7},{7,6},{8,9},{9,8},{10,11... | collective-permute-start | bytes 786440 | tf_op jit(solution)/shard_map/ppermute | solution.py:108
  63.7 1.1 %collective-permute-done.4 = f32[8,8,1024]{2,1,0:T(8,128)S(1)} collective-permute-done((f32[8,8,1024]{2,1,0:T(8,128)S(1)}, f32[8,8,1024]{2,1,0:T(8,128)S(1)}, u32[]{:S(2)}, u32[]{:S(2)}) %collective-permute-start.4) | collective-permute-done | bytes 262176 | tf_op jit(solution)/shard_map/ppermute | solution.py:108
  64.9 37.2 %all_to_all.10 = f32[8,8,1024]{2,1,0:T(8,128)S(1)} all-to-all(f32[8,8,1024]{2,1,0:T(8,128)S(1)} %add.7), channel_id=1, replica_groups={{0,2,4,6,8,10,12,14},{1,3,5,7,9,11,13,15},{16,18,20,22,24,26,28,30},{17..., dimensions={0} | all-to-all | bytes 524288 | tf_op jit(solution)/shard_map/all_to_all | solution.py:109
  102.2 0.6 reduce_sum.9
  (3 shorter events, 0.1 us)
Async XLA Ops:
  0.0 30.2 %copy-start = (bf16[1,1,16,256,256]{4,3,2,1,0:T(8,128)(2,1)S(1)}, bf16[1,1,16,256,256]{4,3,2,1,0:T(8,128)(2,1)}, u32[]{:S(2)}) copy-start(bf16[1,1,16,256,256]{4,3,2,1,0:T(8,128)(2,1)} %param.5) | copy-start | bytes 6291460
  1.6 27.8 %all-to-all-start = ((bf16[16,8,1024]{2,1,0:T(8,128)(2,1)}), bf16[16,8,1024]{2,1,0:T(8,128)(2,1)S(1)}, u32[]{:S(2)}, u32[]{:S(2)}) async-start(bf16[16,8,1024]{2,1,0:T(8,128)(2,1)} %broadcast_in_dim.29), calls=%async_computation | async-start | bytes 524288 | tf_op jit(solution)/shard_map/all_to_all | solution.py:75
  15.5 26.8 %collective-permute-start = (s32[16,16]{1,0:T(8,128)S(1)}, s32[16,16]{1,0:T(8,128)S(1)}, u32[]{:S(2)}, u32[]{:S(2)}) collective-permute-start(s32[16,16]{1,0:T(8,128)S(1)} %broadcast_in_dim.25), channel_id=1, source_target_pairs={{0,6},{1,23},{2,36},{3,54},{4,66},{5,86},{6,104},{7,123},{8,131},{... | collective-permute-start | bytes 3080 | tf_op jit(solution)/shard_map/ppermute | solution.py:73
  30.8 24.1 %collective-permute-start.2 = (f32[16,8,256]{2,1,0:T(8,128)S(1)}, f32[16,8,256]{2,1,0:T(8,128)S(1)}, u32[]{:S(2)}, u32[]{:S(2)}) collective-permute-start(f32[16,8,256]{2,1,0:T(8,128)S(1)} %fusion.4), channel_id=1, source_target_pairs={{0,6},{1,23},{2,36},{3,54},{4,66},{5,86},{6,104},{7,123},{16,18},{... | collective-permute-start | bytes 393224 | tf_op jit(solution)/shard_map/ppermute | solution.py:88
  43.6 11.3 %collective-permute-start.1 = (bf16[16,8,256]{2,1,0:T(8,128)(2,1)S(1)}, bf16[16,8,256]{2,1,0:T(8,128)(2,1)S(1)}, u32[]{:S(2)}, u32[]{:S(2)}) collective-permute-start(bf16[16,8,256]{2,1,0:T(8,128)(2,1)S(1)} %shard_map.47), channel_id=1, source_target_pairs={{6,0},{23,1},{36,2},{54,3},{66,4},{86,5},{104,6},{123,7},{131,8},{... | collective-permute-start | bytes 196616 | tf_op jit(solution)/shard_map/ppermute | solution.py:91
  53.0 2.3 %collective-permute-start.3 = (f32[16,8,256]{2,1,0:T(8,128)S(1)}, f32[16,8,256]{2,1,0:T(8,128)S(1)}, u32[]{:S(2)}, u32[]{:S(2)}) collective-permute-start(f32[16,8,256]{2,1,0:T(8,128)S(1)} %fusion.4), channel_id=1, source_target_pairs={{8,131},{9,144},{10,161},{11,178},{12,205},{13,217},{14,237},{15,2... | collective-permute-start | bytes 393224 | tf_op jit(solution)/shard_map/ppermute | solution.py:93
  56.5 8.4 %collective-permute-start.4 = (f32[8,8,1024]{2,1,0:T(8,128)S(1)}, f32[8,8,1024]{2,1,0:T(8,128)S(1)}, u32[]{:S(2)}, u32[]{:S(2)}) collective-permute-start(f32[8,8,1024]{2,1,0:T(8,128)S(1)} %get-tuple-element.16), channel_id=1, source_target_pairs={{0,1},{1,0},{2,3},{3,2},{4,5},{5,4},{6,7},{7,6},{8,9},{9,8},{10,11... | collective-permute-start | bytes 786440 | tf_op jit(solution)/shard_map/ppermute | solution.py:108

commit v5 on v4

--- a/solution.py
+++ b/solution.py
@@ -68,7 +68,7 @@
 
     def slack(tile, server):
         part = [device // col_count // 4 % 4 for device in (tile, server)]
-        return part[1] == 2 or (part[0] == 0 and part[1] == 3)
+        return part[0] == 0 and part[1] >= 2
 
     far_index = lax.ppermute(jnp.broadcast_to(pair_rows, (16, slots)), both, up)[0]
     copies = jnp.broadcast_to(vectors, (col_count, vec_count, piece))

time: 103 us -> 104 us (level)
  no operation moved by 1% of the time
where the time goes in v5:
time: 104 us; the launch traced here: 103 us
  blocking collectives  37.7 us (36%)
  starting transfers between devices  36.9 us (35%)
  waiting for transfers between devices  20.2 us (19%)
  local copies, waits for them, and re-layouts  3.37 us (3%)
  Pallas kernels  2.68 us (3%)
    all_to_all x1, blocking collectives, body(): lax.all_to_all(total, 'col', 0, 0, axis_index_groups=groups, tiled=True)  37.7 us
    all_to_all x1, starting transfers between devices, body(): segment = lax.all_to_all(copies, 'col', 0, 0, tiled=True)  12.6 us
    ppermute x1, starting transfers between devices, body(): far_rows = lax.ppermute(far_picked, both, down)  9.45 us
    all_to_all x1, waiting for transfers between devices, body(): segment = lax.all_to_all(copies, 'col', 0, 0, tiled=True)  9.41 us
    ppermute x1, waiting for transfers between devices, body(): lax.ppermute(jnp.broadcast_to(pair_rows, (16, slots)), both, up)[0]  8.41 us
    ppermute x1, starting transfers between devices, body(): total = keep + lax.ppermute(send, 'col', swap)  7.27 us
    ppermute x1, starting transfers between devices, body(): lax.ppermute(jnp.broadcast_to(pair_rows, (16, slots)), both, up)[0]  3.82 us
    ppermute x1, starting transfers between devices, body(): lax.ppermute(normal, both, [(a, b) for a, b in up if not slack(a, b)])  3.04 us
  transfers between devices with their start and end apart: 6, of which 4 were waited for; matrix products, arithmetic and copies ran while one was open for 3% of the time, Pallas kernels for 2%

profile of v5, /device:TPU:10, one launch (start us, length us, event | category | flops | bytes accessed | tf_op | source)
XLA Modules:
  0.0 103.2 jit_solution(1523754885055463501)
XLA Ops:
  0.0 0.0 copy-start
  0.0 1.6 %broadcast_in_dim.29 = bf16[16,8,1024]{2,1,0:T(8,128)(2,1)} broadcast(bf16[8,1024]{1,0:T(8,128)(2,1)} %param.4), dimensions={1,2} | broadcast | bytes 278528 | tf_op jit(solution)/shard_map/broadcast_in_dim | solution.py:74
  1.6 12.6 %all-to-all-start = ((bf16[16,8,1024]{2,1,0:T(8,128)(2,1)}), bf16[16,8,1024]{2,1,0:T(8,128)(2,1)S(1)}, u32[]{:S(2)}, u32[]{:S(2)}) async-start(bf16[16,8,1024]{2,1,0:T(8,128)(2,1)} %broadcast_in_dim.29), calls=%async_computation | async-start | bytes 524288 | tf_op jit(solution)/shard_map/all_to_all | solution.py:75
  14.2 1.3 %slice_bitcast_fusion.1 = (s32[16]{0:T(128)S(1)}, s32[16]{0:T(128)}) fusion(s32[1,1,16,2]{2,3,1,0:T(2,128)} %param.6), kind=kLoop, calls=%fused_computation.7 | loop fusion | bytes 256 | tf_op jit(solution)/shard_map/squeeze | solution.py:55
  15.5 3.8 %collective-permute-start = (s32[16,16]{1,0:T(8,128)S(1)}, s32[16,16]{1,0:T(8,128)S(1)}, u32[]{:S(2)}, u32[]{:S(2)}) collective-permute-start(s32[16,16]{1,0:T(8,128)S(1)} %broadcast_in_dim.25), channel_id=1, source_target_pairs={{0,6},{1,23},{2,36},{3,54},{4,66},{5,86},{6,104},{7,123},{8,131},{... | collective-permute-start | bytes 3080 | tf_op jit(solution)/shard_map/ppermute | solution.py:73
  20.0 9.4 %all-to-all-done.segment = bf16[16,8,1024]{2,1,0:T(8,128)(2,1)S(1)} async-done(((bf16[16,8,1024]{2,1,0:T(8,128)(2,1)}), bf16[16,8,1024]{2,1,0:T(8,128)(2,1)S(1)}, u32[]{:S(2)}, u32[]{:S(2)}) %all-to-all-start) | async-done | bytes 262176 | tf_op jit(solution)/shard_map/all_to_all | solution.py:75
  29.4 0.8 shard_map.46
  30.2 0.0 copy-done
  30.2 0.6 fusion.4
  30.8 3.0 %collective-permute-start.2 = (f32[16,8,256]{2,1,0:T(8,128)S(1)}, f32[16,8,256]{2,1,0:T(8,128)S(1)}, u32[]{:S(2)}, u32[]{:S(2)}) collective-permute-start(f32[16,8,256]{2,1,0:T(8,128)S(1)} %fusion.4), channel_id=1, source_target_pairs={{0,6},{1,23},{2,36},{3,54},{4,66},{5,86},{6,104},{7,123},{16,18},{... | collective-permute-start | bytes 393224 | tf_op jit(solution)/shard_map/ppermute | solution.py:88
  33.9 8.4 %collective-permute-done = s32[16,16]{1,0:T(8,128)S(1)} collective-permute-done((s32[16,16]{1,0:T(8,128)S(1)}, s32[16,16]{1,0:T(8,128)S(1)}, u32[]{:S(2)}, u32[]{:S(2)}) %collective-permute-start) | collective-permute-done | bytes 1056 | tf_op jit(solution)/shard_map/ppermute | solution.py:73
  42.3 0.5 slice_bitcast_fusion.index.far_index
  42.8 0.8 shard_map.47
  43.6 9.5 %collective-permute-start.1 = (bf16[16,8,256]{2,1,0:T(8,128)(2,1)S(1)}, bf16[16,8,256]{2,1,0:T(8,128)(2,1)S(1)}, u32[]{:S(2)}, u32[]{:S(2)}) collective-permute-start(bf16[16,8,256]{2,1,0:T(8,128)(2,1)S(1)} %shard_map.47), channel_id=1, source_target_pairs={{6,0},{23,1},{36,2},{54,3},{66,4},{86,5},{104,6},{123,7},{131,8},{... | collective-permute-start | bytes 196616 | tf_op jit(solution)/shard_map/ppermute | solution.py:91
  53.0 0.7 collective-permute-start.3
  53.7 1.2 %collective-permute-done.1 = bf16[16,8,256]{2,1,0:T(8,128)(2,1)S(1)} collective-permute-done((bf16[16,8,256]{2,1,0:T(8,128)(2,1)S(1)}, bf16[16,8,256]{2,1,0:T(8,128)(2,1)S(1)}, u32[]{:S(2)}, u32[]{:S(2)}) %collective-permute-start.1) | collective-permute-done | bytes 65568 | tf_op jit(solution)/shard_map/ppermute | solution.py:91
  54.9 0.0 collective-permute-done.2.arrived
  54.9 0.4 fusion.trans
  55.3 0.0 collective-permute-done.3.late
  55.3 1.1 %shard_map.48 = (f32[8,8,1024]{2,1,0:T(8,128)S(1)}, f32[8,8,1024]{2,1,0:T(8,128)S(1)}) custom-call(s32[16]{0:T(128)} %get-tuple-element.18.index, s32[16]{0:T(128)} %slice_bitcast_fusion.index.far_index, s32[1]{0:T(128)} %bitcast.3.own_ref, s32[1]{0:T(128)} %bitcast.5.count_ref, f32[16,8,256]{2,1,0:T(8,128)S(1)} %fusion.trans, ...), custom_call_target="tpu_custom_call" | custom-call | bytes 1000000 | tf_op jit(solution)/shard_map/pallas_call | solution.py:99
  56.5 7.3 %collective-permute-start.4 = (f32[8,8,1024]{2,1,0:T(8,128)S(1)}, f32[8,8,1024]{2,1,0:T(8,128)S(1)}, u32[]{:S(2)}, u32[]{:S(2)}) collective-permute-start(f32[8,8,1024]{2,1,0:T(8,128)S(1)} %get-tuple-element.16), channel_id=1, source_target_pairs={{0,1},{1,0},{2,3},{3,2},{4,5},{5,4},{6,7},{7,6},{8,9},{9,8},{10,11... | collective-permute-start | bytes 786440 | tf_op jit(solution)/shard_map/ppermute | solution.py:108
  63.7 1.1 %collective-permute-done.4 = f32[8,8,1024]{2,1,0:T(8,128)S(1)} collective-permute-done((f32[8,8,1024]{2,1,0:T(8,128)S(1)}, f32[8,8,1024]{2,1,0:T(8,128)S(1)}, u32[]{:S(2)}, u32[]{:S(2)}) %collective-permute-start.4) | collective-permute-done | bytes 262176 | tf_op jit(solution)/shard_map/ppermute | solution.py:108
  64.9 37.7 %all_to_all.10 = f32[8,8,1024]{2,1,0:T(8,128)S(1)} all-to-all(f32[8,8,1024]{2,1,0:T(8,128)S(1)} %add.7), channel_id=1, replica_groups={{0,2,4,6,8,10,12,14},{1,3,5,7,9,11,13,15},{16,18,20,22,24,26,28,30},{17..., dimensions={0} | all-to-all | bytes 524288 | tf_op jit(solution)/shard_map/all_to_all | solution.py:109
  102.6 0.6 reduce_sum.9
  (3 shorter events, 0.1 us)
Async XLA Ops:
  0.0 30.2 %copy-start = (bf16[1,1,16,256,256]{4,3,2,1,0:T(8,128)(2,1)S(1)}, bf16[1,1,16,256,256]{4,3,2,1,0:T(8,128)(2,1)}, u32[]{:S(2)}) copy-start(bf16[1,1,16,256,256]{4,3,2,1,0:T(8,128)(2,1)} %param.5) | copy-start | bytes 6291460
  1.6 27.8 %all-to-all-start = ((bf16[16,8,1024]{2,1,0:T(8,128)(2,1)}), bf16[16,8,1024]{2,1,0:T(8,128)(2,1)S(1)}, u32[]{:S(2)}, u32[]{:S(2)}) async-start(bf16[16,8,1024]{2,1,0:T(8,128)(2,1)} %broadcast_in_dim.29), calls=%async_computation | async-start | bytes 524288 | tf_op jit(solution)/shard_map/all_to_all | solution.py:75
  15.5 26.8 %collective-permute-start = (s32[16,16]{1,0:T(8,128)S(1)}, s32[16,16]{1,0:T(8,128)S(1)}, u32[]{:S(2)}, u32[]{:S(2)}) collective-permute-start(s32[16,16]{1,0:T(8,128)S(1)} %broadcast_in_dim.25), channel_id=1, source_target_pairs={{0,6},{1,23},{2,36},{3,54},{4,66},{5,86},{6,104},{7,123},{8,131},{... | collective-permute-start | bytes 3080 | tf_op jit(solution)/shard_map/ppermute | solution.py:73
  30.8 24.1 %collective-permute-start.2 = (f32[16,8,256]{2,1,0:T(8,128)S(1)}, f32[16,8,256]{2,1,0:T(8,128)S(1)}, u32[]{:S(2)}, u32[]{:S(2)}) collective-permute-start(f32[16,8,256]{2,1,0:T(8,128)S(1)} %fusion.4), channel_id=1, source_target_pairs={{0,6},{1,23},{2,36},{3,54},{4,66},{5,86},{6,104},{7,123},{16,18},{... | collective-permute-start | bytes 393224 | tf_op jit(solution)/shard_map/ppermute | solution.py:88
  43.6 11.3 %collective-permute-start.1 = (bf16[16,8,256]{2,1,0:T(8,128)(2,1)S(1)}, bf16[16,8,256]{2,1,0:T(8,128)(2,1)S(1)}, u32[]{:S(2)}, u32[]{:S(2)}) collective-permute-start(bf16[16,8,256]{2,1,0:T(8,128)(2,1)S(1)} %shard_map.47), channel_id=1, source_target_pairs={{6,0},{23,1},{36,2},{54,3},{66,4},{86,5},{104,6},{123,7},{131,8},{... | collective-permute-start | bytes 196616 | tf_op jit(solution)/shard_map/ppermute | solution.py:91
  53.0 2.3 %collective-permute-start.3 = (f32[16,8,256]{2,1,0:T(8,128)S(1)}, f32[16,8,256]{2,1,0:T(8,128)S(1)}, u32[]{:S(2)}, u32[]{:S(2)}) collective-permute-start(f32[16,8,256]{2,1,0:T(8,128)S(1)} %fusion.4), channel_id=1, source_target_pairs={{8,131},{9,144},{10,161},{11,178},{12,205},{13,217},{14,237},{15,2... | collective-permute-start | bytes 393224 | tf_op jit(solution)/shard_map/ppermute | solution.py:93
  56.5 8.4 %collective-permute-start.4 = (f32[8,8,1024]{2,1,0:T(8,128)S(1)}, f32[8,8,1024]{2,1,0:T(8,128)S(1)}, u32[]{:S(2)}, u32[]{:S(2)}) collective-permute-start(f32[8,8,1024]{2,1,0:T(8,128)S(1)} %get-tuple-element.16), channel_id=1, source_target_pairs={{0,1},{1,0},{2,3},{3,2},{4,5},{5,4},{6,7},{7,6},{8,9},{9,8},{10,11... | collective-permute-start | bytes 786440 | tf_op jit(solution)/shard_map/ppermute | solution.py:108
